TPU v7x, 32 devices: a whole 2x2x4 slice. The times are simulated.
32 devices in a mesh: seq: 8 (over z, x), grp: 4 (over y, core).
Axes of the slice: x: 2, y: 2, z: 4, core: 2. Of those that a mesh axis runs over, the one named last changes fastest.
Arguments:
- dec_in: bfloat16 [64, 256, 768], P(('seq', 'grp')), may hold values from -6 to 6
- memory: bfloat16 [64, 896, 768], P('grp', 'seq'), may hold values from -6 to 6
- cotangent: bfloat16 [64, 256, 768], P(('seq', 'grp')), may hold values from -6 to 6
- dec_len: int32 [64], P(('seq', 'grp')), may hold values from 1 to 256, as said below
- task_prefix: int32 [64], P(('seq', 'grp')), may hold values from 0 to 128
- owner: int32 [4, 16], replicated, may hold values from 0 to 15, each once within a row
- mem_len: int32 [64], replicated, may hold values from 224 to 896, as said below
- self_norm_gain: bfloat16 [768], replicated, may hold values from 0.5 to 1.5
- self_norm_shift: bfloat16 [768], replicated, may hold values from -1.75 to 1.75
- self_qkv: bfloat16 [768, 2304], replicated, may hold values from -0.21875 to 0.21875
- self_q_bias: bfloat16 [768], replicated, may hold values from -1.75 to 1.75
- self_v_bias: bfloat16 [768], replicated, may hold values from -1.75 to 1.75
- rel_bias_table: bfloat16 [64, 12], replicated, may hold values from -6 to 6
- self_head_gain: bfloat16 [12], replicated, may hold values from 0.5 to 1.5
- self_mix_gain: bfloat16 [768], replicated, may hold values from 0.5 to 1.5
- self_mix_shift: bfloat16 [768], replicated, may hold values from -1.75 to 1.75
- self_out: bfloat16 [768, 768], replicated, may hold values from -0.21875 to 0.21875
- self_out_bias: bfloat16 [768], replicated, may hold values from -1.75 to 1.75
- cross_norm_gain: bfloat16 [768], replicated, may hold values from 0.5 to 1.5
- cross_norm_shift: bfloat16 [768], replicated, may hold values from -1.75 to 1.75
- cross_q: bfloat16 [768, 768], replicated, may hold values from -0.21875 to 0.21875
- cross_q_bias: bfloat16 [768], replicated, may hold values from -1.75 to 1.75
- cross_kv: bfloat16 [768, 1536], replicated, may hold values from -0.21875 to 0.21875
- cross_v_bias: bfloat16 [768], replicated, may hold values from -1.75 to 1.75
- cross_head_gain: bfloat16 [12], replicated, may hold values from 0.5 to 1.5
- cross_mix_gain: bfloat16 [768], replicated, may hold values from 0.5 to 1.5
- cross_mix_shift: bfloat16 [768], replicated, may hold values from -1.75 to 1.75
- cross_out: bfloat16 [768, 768], replicated, may hold values from -0.21875 to 0.21875
- cross_out_bias: bfloat16 [768], replicated, may hold values from -1.75 to 1.75
- ffn_norm_gain: bfloat16 [768], replicated, may hold values from 0.5 to 1.5
- ffn_norm_shift: bfloat16 [768], replicated, may hold values from -1.75 to 1.75
- ffn_in: bfloat16 [768, 3072], replicated, may hold values from -0.21875 to 0.21875
- ffn_in_bias: bfloat16 [3072], replicated, may hold values from -1.75 to 1.75
- ffn_mid_gain: bfloat16 [3072], replicated, may hold values from 0.5 to 1.5
- ffn_mid_shift: bfloat16 [3072], replicated, may hold values from -1.75 to 1.75
- ffn_out: bfloat16 [3072, 768], replicated, may hold values from -0.109375 to 0.109375
- ffn_out_bias: bfloat16 [768], replicated, may hold values from -1.75 to 1.75
Outputs:
- out: bfloat16 [64, 256, 768], P(('seq', 'grp'))
- grad_dec_in: bfloat16 [64, 256, 768], P(('seq', 'grp'))
- grad_memory: bfloat16 [64, 896, 768], P('grp', 'seq')
- grad_self_norm_gain: float32 [768], P('grp')
- grad_self_norm_shift: float32 [768], P('grp')
- grad_self_qkv: float32 [768, 2304], P('grp')
- grad_self_q_bias: float32 [768], P('grp')
- grad_self_v_bias: float32 [768], P('grp')
- grad_rel_bias_table: float32 [64, 12], P('grp')
- grad_self_head_gain: float32 [12], P('grp')
- grad_self_mix_gain: float32 [768], P('grp')
- grad_self_mix_shift: float32 [768], P('grp')
- grad_self_out: float32 [768, 768], P('grp')
- grad_self_out_bias: float32 [768], P('grp')
- grad_cross_norm_gain: float32 [768], P('grp')
- grad_cross_norm_shift: float32 [768], P('grp')
- grad_cross_q: float32 [768, 768], P('grp')
- grad_cross_q_bias: float32 [768], P('grp')
- grad_cross_kv: float32 [768, 1536], P('grp')
- grad_cross_v_bias: float32 [768], P('grp')
- grad_cross_head_gain: float32 [12], P('grp')
- grad_cross_mix_gain: float32 [768], P('grp')
- grad_cross_mix_shift: float32 [768], P('grp')
- grad_cross_out: float32 [768, 768], P('grp')
- grad_cross_out_bias: float32 [768], P('grp')
- grad_ffn_norm_gain: float32 [768], P('grp')
- grad_ffn_norm_shift: float32 [768], P('grp')
- grad_ffn_in: float32 [768, 3072], P('grp')
- grad_ffn_in_bias: float32 [3072], P('grp')
- grad_ffn_mid_gain: float32 [3072], P('grp')
- grad_ffn_mid_shift: float32 [3072], P('grp')
- grad_ffn_out: float32 [3072, 768], P('grp')
- grad_ffn_out_bias: float32 [768], P('grp')
Inputs may be any that keep to these rules, and one draw needn't show every extreme that they name: `dec_len`: in every draw some item has exactly 256 decoder tokens. `mem_len`: in every draw one memory item of each group of 16 has all 896 tokens valid.
All inputs are finite; a program needn't handle non-finite values.
Results may differ from a plain program's by a relative error of at most 0.018.
Values may be sent and summed in bfloat16 or wider, within the bound.
No kernel may reach another device: no remote copies, remote signals or barrier semaphores. Data moves between devices by JAX's collectives and lax.ppermute only.
A program may use at most 256 MiB of HBM per device.

v0:
```python
import math

import jax
import jax.numpy as jnp
from jax import lax
from jax.sharding import PartitionSpec as P

H = 12
HD = 64


EPSILON = 1e-05
PRECISE = lax.Precision.HIGHEST


def layer_norm(values, scaling, offset):
    average = jnp.mean(values, axis=-1, keepdims=True)
    centered = values - average
    spread = jnp.mean(centered * centered, axis=-1, keepdims=True)
    return centered * lax.rsqrt(spread + EPSILON) * scaling + offset


def activate(hidden, scaling, offset):
    return layer_norm(jax.nn.gelu(hidden, approximate=False), scaling, offset)


def rows_dot(left, right):
    return jnp.dot(left, right, preferred_element_type=jnp.float32)


def left_dot(left, right):
    return lax.dot_general(
        left, right, (((0,), (0,)), ((), ())), preferred_element_type=jnp.float32
    )


def right_dot(left, right):
    return lax.dot_general(
        left, right, (((1,), (1,)), ((), ())), preferred_element_type=jnp.float32
    )


def column_sum(values):
    return jnp.sum(values.astype(jnp.float32), axis=0)


def score_block(queries, keys, bias, allowed, factor):
    scores = (
        jnp.einsum("iqhd,ikhd->ihqk", queries, keys, preferred_element_type=jnp.float32) * factor
    )
    if bias is not None:
        scores = scores + bias[None]
    return jnp.where(allowed[:, None], scores, -1000000000.0)


def attend(queries, keys, values, bias, allowed, factor):
    scores = score_block(queries, keys, bias, allowed, factor)
    peak = jnp.max(scores, axis=-1, keepdims=True)
    weights = jnp.exp(scores - peak)
    total = jnp.sum(weights, axis=-1, keepdims=True)
    probs = (weights / total).astype(jnp.bfloat16)
    mixed = jnp.einsum("ihqk,ikhd->iqhd", probs, values, preferred_element_type=jnp.float32)
    return (mixed, peak + jnp.log(total))


def attend_back(queries, keys, values, bias, allowed, factor, logsum, grad_mixed):
    scores = score_block(queries, keys, bias, allowed, factor)
    probs = jnp.exp(scores - logsum)
    grad_probs = jnp.einsum(
        "iqhd,ikhd->ihqk", grad_mixed, values, preferred_element_type=jnp.float32
    )
    grad_scores = probs * (grad_probs - jnp.sum(probs * grad_probs, axis=-1, keepdims=True))
    low_scores = grad_scores.astype(jnp.bfloat16)
    grad_queries = (
        jnp.einsum("ihqk,ikhd->iqhd", low_scores, keys, preferred_element_type=jnp.float32) * factor
    )
    grad_keys = (
        jnp.einsum("ihqk,iqhd->ikhd", low_scores, queries, preferred_element_type=jnp.float32)
        * factor
    )
    grad_values = jnp.einsum(
        "ihqk,iqhd->ikhd",
        probs.astype(jnp.bfloat16),
        grad_mixed,
        preferred_element_type=jnp.float32,
    )
    return (grad_queries, grad_keys, grad_values, low_scores)


def local(
    dec_in,
    memory,
    cotangent,
    dec_len,
    task_prefix,
    owner,
    mem_len,
    self_norm_gain,
    self_norm_shift,
    self_qkv,
    self_q_bias,
    self_v_bias,
    rel_bias_table,
    self_head_gain,
    self_mix_gain,
    self_mix_shift,
    self_out,
    self_out_bias,
    cross_norm_gain,
    cross_norm_shift,
    cross_q,
    cross_q_bias,
    cross_kv,
    cross_v_bias,
    cross_head_gain,
    cross_mix_gain,
    cross_mix_shift,
    cross_out,
    cross_out_bias,
    ffn_norm_gain,
    ffn_norm_shift,
    ffn_in,
    ffn_in_bias,
    ffn_mid_gain,
    ffn_mid_shift,
    ffn_out,
    ffn_out_bias,
):
    items, length, width = dec_in.shape
    rows = items * length
    items_grp = owner.shape[1]
    shard_tokens = memory.shape[1]
    mem_tokens = shard_tokens * lax.axis_size("seq")
    factor = 1.0 / math.sqrt(HD)
    group = lax.axis_index("grp")
    seq_index = lax.axis_index("seq")
    owner_row = lax.dynamic_index_in_dim(owner, group, 0, keepdims=False)
    inverse = (
        jnp.zeros((items_grp,), jnp.int32).at[owner_row].set(jnp.arange(items_grp, dtype=jnp.int32))
    )
    mine = lax.dynamic_slice_in_dim(inverse, seq_index * items, items)
    my_mem_len = jnp.take(mem_len, group * items_grp + mine)
    positions = jnp.arange(length, dtype=jnp.int32)
    query_pos = positions[None, :, None]
    key_pos = positions[None, None, :]
    self_allowed = (key_pos < dec_len[:, None, None]) & (
        (key_pos <= query_pos) | (key_pos < task_prefix[:, None, None])
    )
    cross_allowed = (
        jnp.arange(mem_tokens, dtype=jnp.int32)[None, None, :] < my_mem_len[:, None, None]
    )
    bucket_count = rel_bias_table.shape[0]
    buckets = (
        jnp.clip(
            positions[None, :] - positions[:, None], -(bucket_count // 2), bucket_count // 2 - 1
        )
        + bucket_count // 2
    )
    one_hot = (
        buckets.reshape(-1)[:, None] == jnp.arange(bucket_count, dtype=jnp.int32)[None, :]
    ).astype(jnp.float32)
    bias = jnp.dot(one_hot, rel_bias_table.astype(jnp.float32), precision=PRECISE).T.reshape(
        H, length, length
    )
    sorted_mem = jnp.take(memory, inverse, axis=0)
    local_rows = sorted_mem.reshape(-1, width)
    kv_proj = rows_dot(local_rows, cross_kv)
    keys_send = kv_proj[:, :width].astype(jnp.bfloat16).reshape(items_grp, shard_tokens, width)
    values_send = (
        (kv_proj[:, width:] + cross_v_bias.astype(jnp.float32))
        .astype(jnp.bfloat16)
        .reshape(items_grp, shard_tokens, width)
    )
    keys_got, values_got = (
        lax.all_to_all(keys_send, "seq", split_axis=0, concat_axis=1, tiled=True),
        lax.all_to_all(values_send, "seq", split_axis=0, concat_axis=1, tiled=True),
    )
    keys_mem = keys_got.reshape(items, mem_tokens, H, HD)
    values_mem = values_got.reshape(items, mem_tokens, H, HD)
    x_rows = dec_in.reshape(rows, width).astype(jnp.float32)
    normed1, pull_norm1 = jax.vjp(
        layer_norm, x_rows, self_norm_gain.astype(jnp.float32), self_norm_shift.astype(jnp.float32)
    )
    normed1_low = normed1.astype(jnp.bfloat16)
    projected = rows_dot(normed1_low, self_qkv)
    queries = (
        (projected[:, :width] + self_q_bias.astype(jnp.float32))
        .astype(jnp.bfloat16)
        .reshape(items, length, H, HD)
    )
    keys = projected[:, width : 2 * width].astype(jnp.bfloat16).reshape(items, length, H, HD)
    values = (
        (projected[:, 2 * width :] + self_v_bias.astype(jnp.float32))
        .astype(jnp.bfloat16)
        .reshape(items, length, H, HD)
    )
    mixed1, logsum1 = attend(queries, keys, values, bias, self_allowed, factor)
    mixed1_rows = mixed1.reshape(rows, H, HD)
    head1 = self_head_gain.astype(jnp.float32)
    scaled1 = (mixed1_rows * head1[None, :, None]).reshape(rows, width)
    mix1, pull_mix1 = jax.vjp(
        layer_norm, scaled1, self_mix_gain.astype(jnp.float32), self_mix_shift.astype(jnp.float32)
    )
    mix1_low = mix1.astype(jnp.bfloat16)
    after_self = x_rows + rows_dot(mix1_low, self_out) + self_out_bias.astype(jnp.float32)
    normed2, pull_norm2 = jax.vjp(
        layer_norm,
        after_self,
        cross_norm_gain.astype(jnp.float32),
        cross_norm_shift.astype(jnp.float32),
    )
    normed2_low = normed2.astype(jnp.bfloat16)
    queries2 = (
        (rows_dot(normed2_low, cross_q) + cross_q_bias.astype(jnp.float32))
        .astype(jnp.bfloat16)
        .reshape(items, length, H, HD)
    )
    mixed2, logsum2 = attend(queries2, keys_mem, values_mem, None, cross_allowed, factor)
    mixed2_rows = mixed2.reshape(rows, H, HD)
    head2 = cross_head_gain.astype(jnp.float32)
    scaled2 = (mixed2_rows * head2[None, :, None]).reshape(rows, width)
    mix2, pull_mix2 = jax.vjp(
        layer_norm, scaled2, cross_mix_gain.astype(jnp.float32), cross_mix_shift.astype(jnp.float32)
    )
    mix2_low = mix2.astype(jnp.bfloat16)
    after_cross = after_self + rows_dot(mix2_low, cross_out) + cross_out_bias.astype(jnp.float32)
    normed3, pull_norm3 = jax.vjp(
        layer_norm,
        after_cross,
        ffn_norm_gain.astype(jnp.float32),
        ffn_norm_shift.astype(jnp.float32),
    )
    normed3_low = normed3.astype(jnp.bfloat16)
    hidden = rows_dot(normed3_low, ffn_in) + ffn_in_bias.astype(jnp.float32)
    middle, pull_middle = jax.vjp(
        activate, hidden, ffn_mid_gain.astype(jnp.float32), ffn_mid_shift.astype(jnp.float32)
    )
    middle_low = middle.astype(jnp.bfloat16)
    result = after_cross + rows_dot(middle_low, ffn_out) + ffn_out_bias.astype(jnp.float32)
    out = result.astype(jnp.bfloat16).reshape(items, length, width)
    valid = (positions[None, :] < dec_len[:, None]).astype(jnp.float32).reshape(rows, 1)
    grad_out = cotangent.reshape(rows, width).astype(jnp.float32) * valid
    grad_low = grad_out.astype(jnp.bfloat16)
    grad_ffn_out = left_dot(middle_low, grad_low)
    grad_ffn_out_bias = column_sum(grad_low)
    grad_hidden, grad_ffn_mid_gain, grad_ffn_mid_shift = pull_middle(right_dot(grad_low, ffn_out))
    hidden_low = grad_hidden.astype(jnp.bfloat16)
    grad_ffn_in = left_dot(normed3_low, hidden_low)
    grad_ffn_in_bias = column_sum(hidden_low)
    grad_part3, grad_ffn_norm_gain, grad_ffn_norm_shift = pull_norm3(right_dot(hidden_low, ffn_in))
    grad_x3 = grad_part3 + grad_out
    branch_low = grad_x3.astype(jnp.bfloat16)
    grad_cross_out = left_dot(mix2_low, branch_low)
    grad_cross_out_bias = column_sum(branch_low)
    grad_scaled2, grad_cross_mix_gain, grad_cross_mix_shift = pull_mix2(
        right_dot(branch_low, cross_out)
    )
    grad_scaled2 = grad_scaled2.reshape(rows, H, HD)
    grad_cross_head_gain = jnp.sum(grad_scaled2 * mixed2_rows, axis=(0, 2))
    grad_mixed2 = (
        (grad_scaled2 * head2[None, :, None]).astype(jnp.bfloat16).reshape(items, length, H, HD)
    )
    grad_q2, grad_k2, grad_v2, cross_score_grads = attend_back(
        queries2, keys_mem, values_mem, None, cross_allowed, factor, logsum2, grad_mixed2
    )
    q2_low = grad_q2.reshape(rows, width).astype(jnp.bfloat16)
    grad_cross_q = left_dot(normed2_low, q2_low)
    grad_cross_q_bias = column_sum(q2_low)
    grad_part2, grad_cross_norm_gain, grad_cross_norm_shift = pull_norm2(right_dot(q2_low, cross_q))
    grad_x2 = grad_part2 + grad_x3
    keys_low = grad_k2.reshape(items, mem_tokens, width).astype(jnp.bfloat16)
    values_low = grad_v2.reshape(items, mem_tokens, width).astype(jnp.bfloat16)
    back_keys, back_values = (
        lax.all_to_all(keys_low, "seq", split_axis=1, concat_axis=0, tiled=True),
        lax.all_to_all(values_low, "seq", split_axis=1, concat_axis=0, tiled=True),
    )
    kv_rows = jnp.concatenate([back_keys, back_values], axis=2).reshape(-1, 2 * width)
    grad_cross_kv = left_dot(local_rows, kv_rows)
    grad_cross_v_bias = column_sum(kv_rows[:, width:])
    grad_mem = right_dot(kv_rows, cross_kv).reshape(items_grp, shard_tokens, width)
    grad_memory = jnp.take(grad_mem, owner_row, axis=0).astype(jnp.bfloat16)
    branch_low = grad_x2.astype(jnp.bfloat16)
    grad_self_out = left_dot(mix1_low, branch_low)
    grad_self_out_bias = column_sum(branch_low)
    grad_scaled1, grad_self_mix_gain, grad_self_mix_shift = pull_mix1(
        right_dot(branch_low, self_out)
    )
    grad_scaled1 = grad_scaled1.reshape(rows, H, HD)
    grad_self_head_gain = jnp.sum(grad_scaled1 * mixed1_rows, axis=(0, 2))
    grad_mixed1 = (
        (grad_scaled1 * head1[None, :, None]).astype(jnp.bfloat16).reshape(items, length, H, HD)
    )
    grad_q, grad_k, grad_v, score_grads = attend_back(
        queries, keys, values, bias, self_allowed, factor, logsum1, grad_mixed1
    )
    summed = jnp.sum(score_grads.astype(jnp.float32), axis=0).reshape(H, length * length)
    grad_rel_bias_table = jnp.dot(summed, one_hot, precision=PRECISE).T
    qkv_low = jnp.concatenate(
        [grad_q.reshape(rows, width), grad_k.reshape(rows, width), grad_v.reshape(rows, width)],
        axis=1,
    ).astype(jnp.bfloat16)
    grad_self_qkv = left_dot(normed1_low, qkv_low)
    grad_self_q_bias = column_sum(qkv_low[:, :width])
    grad_self_v_bias = column_sum(qkv_low[:, 2 * width :])
    grad_part1, grad_self_norm_gain, grad_self_norm_shift = pull_norm1(right_dot(qkv_low, self_qkv))
    grad_dec_in = (grad_part1 + grad_x2).astype(jnp.bfloat16).reshape(items, length, width)
    local_grads = (
        grad_self_norm_gain,
        grad_self_norm_shift,
        grad_self_qkv,
        grad_self_q_bias,
        grad_self_v_bias,
        grad_rel_bias_table,
        grad_self_head_gain,
        grad_self_mix_gain,
        grad_self_mix_shift,
        grad_self_out,
        grad_self_out_bias,
        grad_cross_norm_gain,
        grad_cross_norm_shift,
        grad_cross_q,
        grad_cross_q_bias,
        grad_cross_kv,
        grad_cross_v_bias,
        grad_cross_head_gain,
        grad_cross_mix_gain,
        grad_cross_mix_shift,
        grad_cross_out,
        grad_cross_out_bias,
        grad_ffn_norm_gain,
        grad_ffn_norm_shift,
        grad_ffn_in,
        grad_ffn_in_bias,
        grad_ffn_mid_gain,
        grad_ffn_mid_shift,
        grad_ffn_out,
        grad_ffn_out_bias,
    )
    shares = (
        lax.psum_scatter(
            local_grads[0].astype(jnp.bfloat16), "grp", scatter_dimension=0, tiled=True
        ).astype(jnp.float32),
        lax.psum_scatter(
            local_grads[1].astype(jnp.bfloat16), "grp", scatter_dimension=0, tiled=True
        ).astype(jnp.float32),
        lax.psum_scatter(
            local_grads[2].astype(jnp.bfloat16), "grp", scatter_dimension=0, tiled=True
        ).astype(jnp.float32),
        lax.psum_scatter(
            local_grads[3].astype(jnp.bfloat16), "grp", scatter_dimension=0, tiled=True
        ).astype(jnp.float32),
        lax.psum_scatter(
            local_grads[4].astype(jnp.bfloat16), "grp", scatter_dimension=0, tiled=True
        ).astype(jnp.float32),
        lax.psum_scatter(
            local_grads[5].astype(jnp.bfloat16), "grp", scatter_dimension=0, tiled=True
        ).astype(jnp.float32),
        lax.psum_scatter(
            local_grads[6].astype(jnp.bfloat16), "grp", scatter_dimension=0, tiled=True
        ).astype(jnp.float32),
        lax.psum_scatter(
            local_grads[7].astype(jnp.bfloat16), "grp", scatter_dimension=0, tiled=True
        ).astype(jnp.float32),
        lax.psum_scatter(
            local_grads[8].astype(jnp.bfloat16), "grp", scatter_dimension=0, tiled=True
        ).astype(jnp.float32),
        lax.psum_scatter(
            local_grads[9].astype(jnp.bfloat16), "grp", scatter_dimension=0, tiled=True
        ).astype(jnp.float32),
        lax.psum_scatter(
            local_grads[10].astype(jnp.bfloat16), "grp", scatter_dimension=0, tiled=True
        ).astype(jnp.float32),
        lax.psum_scatter(
            local_grads[11].astype(jnp.bfloat16), "grp", scatter_dimension=0, tiled=True
        ).astype(jnp.float32),
        lax.psum_scatter(
            local_grads[12].astype(jnp.bfloat16), "grp", scatter_dimension=0, tiled=True
        ).astype(jnp.float32),
        lax.psum_scatter(
            local_grads[13].astype(jnp.bfloat16), "grp", scatter_dimension=0, tiled=True
        ).astype(jnp.float32),
        lax.psum_scatter(
            local_grads[14].astype(jnp.bfloat16), "grp", scatter_dimension=0, tiled=True
        ).astype(jnp.float32),
        lax.psum_scatter(
            local_grads[15].astype(jnp.bfloat16), "grp", scatter_dimension=0, tiled=True
        ).astype(jnp.float32),
        lax.psum_scatter(
            local_grads[16].astype(jnp.bfloat16), "grp", scatter_dimension=0, tiled=True
        ).astype(jnp.float32),
        lax.psum_scatter(
            local_grads[17].astype(jnp.bfloat16), "grp", scatter_dimension=0, tiled=True
        ).astype(jnp.float32),
        lax.psum_scatter(
            local_grads[18].astype(jnp.bfloat16), "grp", scatter_dimension=0, tiled=True
        ).astype(jnp.float32),
        lax.psum_scatter(
            local_grads[19].astype(jnp.bfloat16), "grp", scatter_dimension=0, tiled=True
        ).astype(jnp.float32),
        lax.psum_scatter(
            local_grads[20].astype(jnp.bfloat16), "grp", scatter_dimension=0, tiled=True
        ).astype(jnp.float32),
        lax.psum_scatter(
            local_grads[21].astype(jnp.bfloat16), "grp", scatter_dimension=0, tiled=True
        ).astype(jnp.float32),
        lax.psum_scatter(
            local_grads[22].astype(jnp.bfloat16), "grp", scatter_dimension=0, tiled=True
        ).astype(jnp.float32),
        lax.psum_scatter(
            local_grads[23].astype(jnp.bfloat16), "grp", scatter_dimension=0, tiled=True
        ).astype(jnp.float32),
        lax.psum_scatter(
            local_grads[24].astype(jnp.bfloat16), "grp", scatter_dimension=0, tiled=True
        ).astype(jnp.float32),
        lax.psum_scatter(
            local_grads[25].astype(jnp.bfloat16), "grp", scatter_dimension=0, tiled=True
        ).astype(jnp.float32),
        lax.psum_scatter(
            local_grads[26].astype(jnp.bfloat16), "grp", scatter_dimension=0, tiled=True
        ).astype(jnp.float32),
        lax.psum_scatter(
            local_grads[27].astype(jnp.bfloat16), "grp", scatter_dimension=0, tiled=True
        ).astype(jnp.float32),
        lax.psum_scatter(
            local_grads[28].astype(jnp.bfloat16), "grp", scatter_dimension=0, tiled=True
        ).astype(jnp.float32),
        lax.psum_scatter(
            local_grads[29].astype(jnp.bfloat16), "grp", scatter_dimension=0, tiled=True
        ).astype(jnp.float32),
    )
    totals = lax.psum(
        (
            shares[0],
            shares[1],
            shares[2],
            shares[3],
            shares[4],
            shares[5],
            shares[6],
            shares[7],
            shares[8],
            shares[9],
            shares[10],
            shares[11],
            shares[12],
            shares[13],
            shares[14],
            shares[15],
            shares[16],
            shares[17],
            shares[18],
            shares[19],
            shares[20],
            shares[21],
            shares[22],
            shares[23],
            shares[24],
            shares[25],
            shares[26],
            shares[27],
            shares[28],
            shares[29],
        ),
        "seq",
    )
    return (out, grad_dec_in, grad_memory) + tuple(totals)


def solution(mesh):
    in_specs = (
        P(("seq", "grp"), None, None),
        P("grp", "seq", None),
        P(("seq", "grp"), None, None),
        P(("seq", "grp")),
        P(("seq", "grp")),
        P(),
        P(),
        P(),
        P(),
        P(),
        P(),
        P(),
        P(),
        P(),
        P(),
        P(),
        P(),
        P(),
        P(),
        P(),
        P(),
        P(),
        P(),
        P(),
        P(),
        P(),
        P(),
        P(),
        P(),
        P(),
        P(),
        P(),
        P(),
        P(),
        P(),
        P(),
        P(),
    )
    out_specs = (
        P(("seq", "grp"), None, None),
        P(("seq", "grp"), None, None),
        P("grp", "seq", None),
        P("grp"),
        P("grp"),
        P("grp", None),
        P("grp"),
        P("grp"),
        P("grp", None),
        P("grp"),
        P("grp"),
        P("grp"),
        P("grp", None),
        P("grp"),
        P("grp"),
        P("grp"),
        P("grp", None),
        P("grp"),
        P("grp", None),
        P("grp"),
        P("grp"),
        P("grp"),
        P("grp"),
        P("grp", None),
        P("grp"),
        P("grp"),
        P("grp"),
        P("grp", None),
        P("grp"),
        P("grp"),
        P("grp"),
        P("grp", None),
        P("grp"),
    )
    return jax.shard_map(local, mesh=mesh, in_specs=in_specs, out_specs=out_specs, check_vma=False)
```

profile of v0, /device:TPU:0, one launch (start us, length us, event | category | flops | bytes accessed | tf_op | source)
XLA Modules:
  0.0 1040.9 jit_solution(15393551780788417120)
XLA Ops:
  9.4 4.0 gather_fusion
  16.0 4.5 fusion.117
  20.5 4.2 copy-done.22
  26.6 7.6 all-to-all-start.1
  99.4 4.5 fusion.18
  103.9 6.0 all-to-all-start
  110.0 3.9 fusion.110
  146.8 4.9 copy.250
  151.7 6.1 reshape.647
  157.8 14.0 %all-to-all-done = bf16[16,112,768]{2,1,0:T(8,128)(2,1)} async-done(((bf16[16,112,768]{2,1,0:T(8,128)(2,1)}), bf16[16,112,768]{2,1,0:T(8,128)(2,1)}, u32[]{:S(2)}, u32[]{:S(2)}) %all-to-all-start) | async-done | bytes 2752544 | tf_op jit(solution)/shard_map/all_to_all | solution.py:176
  171.8 4.9 copy.248
  176.7 6.4 reshape.644
  183.1 12.6 %fusion.8 = (f32[2,12,256]{2,1,0:T(8,128)S(1)}, f32[2,12,256,896]{3,2,1,0:T(8,128)}) fusion(pred[2,896]{1,0:T(4,128)(4,1)S(1)} %iota_compare_fusion.6, bf16[2,896,12,64]{1,3,2,0:T(8,128)(2,1)} %reshape.647, bf16[2,256,12,64]{1,0,3,2:T(2,128)(2,1)} %reshape.645), kind=kOutput, calls=%fused_computation.20 | convolution fusion | flops 721152000 | bytes 25585408 | tf_op jit(solution)/shard_map/iqhd,ikhd->ihqk/dot_general | solution.py:49
  195.8 10.5 %fusion = f32[2,12,256]{2,1,0:T(8,128)S(1)} fusion(f32[2,12,256]{2,1,0:T(8,128)S(1)} %get-tuple-element.149, f32[2,12,256,896]{3,2,1,0:T(8,128)} %get-tuple-element.150, pred[2,896]{1,0:T(4,128)(4,1)S(1)} %iota_compare_fusion.6), kind=kLoop, calls=%fused_computation.10 | loop fusion | flops 22013952 | bytes 22071040 | tf_op jit(solution)/shard_map/reduce_sum | solution.py:60
  206.9 11.0 %multiply_reduce_fusion.19 = (f32[2,256]{1,0:T(2,128)S(1)}, f32[2,256,12,64]{1,3,2,0:T(8,128)S(1)}) fusion(f32[12]{0:T(128)S(1)} %copy-done.85, bf16[2,896,12,64]{1,3,2,0:T(8,128)(2,1)S(1)} %copy-done.13, f32[2,12,256]{2,1,0:T(8,128)S(1)} %fusion, f32[2,12,256]{2,1,0:T(8,128)S(1)} %get-tuple-element.149, f32[2,12,256,896]{3,2,1,0:T(8,128)} %get-tuple-element.150, ...), kind=kOutput, calls=%fused_computation.139 | convolution fusion | flops 732954112 | bytes 26398512 | tf_op jit(solution)/shard_map/ihqk,ikhd->iqhd/dot_general | solution.py:62
  229.4 19.9 %fusion.108 = (f32[512]{0:T(512)S(1)}, f32[512,3072]{1,0:T(8,128)S(1)}, f32[512,3072]{1,0:T(8,128)S(1)}, f32[512,3072]{1,0:T(8,128)}) fusion(f32[3072]{0:T(1024)S(1)} %copy-done.39, bf16[768,3072]{1,0:T(8,128)(2,1)} %param.68, f32[512,768]{1,0:T(8,128)S(1)} %get-tuple-element.154, f32[768]{0:T(1024)S(1)} %copy-done.88, f32[768]{0:T(1024)S(1)} %copy-done.68, ...), kind=kOutput, calls=%fused_computation.261 | convolution fusion | flops 2521693696 | bytes 25190400 | tf_op jit(solution)/shard_map/dot_general | solution.py:28
  249.3 5.8 multiply_reduce_fusion.3
  255.1 5.2 multiply_reduce_fusion.1
  260.3 9.6 fusion.101
  269.9 6.8 multiply_reduce_fusion.5
  290.4 17.4 %multiply_reduce_fusion = (f32[2,12,256]{2,1,0:T(8,128)}, f32[2,12,256,896]{3,2,1,0:T(8,128)}) fusion(f32[2,12,256]{2,1,0:T(8,128)} %log_add_fusion, f32[2,12,256,896]{3,2,1,0:T(8,128)} %get-tuple-element.150, pred[2,896]{1,0:T(4,128)(4,1)S(1)} %iota_compare_fusion.6, bf16[2,896,12,64]{1,3,2,0:T(8,128)(2,1)} %reshape.644, f32[2,256,12,64]{1,0,3,2:T(2,128)} %reshape.650, ...), kind=kOutput, calls=%fused_computation.5 | convolution fusion | flops 732948480 | bytes 48416560 | tf_op jit(solution)/shard_map/iqhd,ikhd->ihqk/dot_general | solution.py:69
  307.8 15.0 %multiply_convert_fusion = bf16[2,12,256,896]{3,2,1,0:T(8,128)(2,1)S(1)} fusion(f32[2,12,256,896]{3,2,1,0:T(8,128)} %get-tuple-element.160, f32[2,12,256]{2,1,0:T(8,128)} %get-tuple-element.159, f32[2,12,256]{2,1,0:T(8,128)} %log_add_fusion, f32[2,12,256,896]{3,2,1,0:T(8,128)} %get-tuple-element.150, pred[2,896]{1,0:T(4,128)(4,1)S(1)} %iota_compare_fusion.6), kind=kLoop, calls=%fused_computation.4 | loop fusion | flops 33030144 | bytes 55101184 | tf_op jit(solution)/shard_map/convert_element_type | solution.py:73
  322.9 8.8 fusion.115
  350.0 5.2 multiply_reduce_fusion.2
  355.2 8.1 convert_reduce_fusion
  371.7 8.5 fusion.60
  388.3 3.9 convolution_convert_fusion.5
  392.4 5.1 fusion.114
  405.6 3.8 convolution_convert_fusion.2
  409.7 7.0 convolution_convert_fusion
  417.3 11.5 %fusion.29 = bf16[2,12,64,896]{3,2,1,0:T(8,128)(2,1)} fusion(f32[2,12,256]{2,1,0:T(8,128)} %log_add_fusion, f32[2,12,256,896]{3,2,1,0:T(8,128)} %get-tuple-element.150, pred[2,896]{1,0:T(4,128)(4,1)S(1)} %iota_compare_fusion.6, f32[2,256,12,64]{1,0,3,2:T(2,128)} %reshape.650, f32[12]{0:T(128)S(1)} %copy-done.87), kind=kOutput, calls=%fused_computation.76 | convolution fusion | flops 728825856 | bytes 26371888 | tf_op jit(solution)/shard_map/ihqk,iqhd->ikhd/dot_general | solution.py:81
  428.8 8.6 copy.272
  437.4 4.6 all-to-all-start.3
  442.1 7.4 convolution_convert_fusion.1
  449.4 7.8 multiply_convert_fusion.2
  457.3 8.6 copy.269
  465.9 38.1 %all-to-all-done.3 = bf16[2,896,768]{2,0,1:T(2,128)(2,1)} async-done(((bf16[2,896,768]{2,0,1:T(2,128)(2,1)}), bf16[2,896,768]{2,0,1:T(2,128)(2,1)}, u32[]{:S(2)}, u32[]{:S(2)}) %all-to-all-start.3) | async-done | bytes 2752544 | tf_op jit(solution)/shard_map/all_to_all | solution.py:275
  504.0 4.4 all-to-all-start.2
  515.4 4.8 fusion.100
  526.1 44.1 %all-to-all-done.2 = bf16[2,896,768]{2,0,1:T(2,128)(2,1)} async-done(((bf16[2,896,768]{2,0,1:T(2,128)(2,1)}), bf16[2,896,768]{2,0,1:T(2,128)(2,1)}, u32[]{:S(2)}, u32[]{:S(2)}) %all-to-all-start.2) | async-done | bytes 2752544 | tf_op jit(solution)/shard_map/all_to_all | solution.py:274
  576.0 6.4 bitcast_convert_fusion
  592.8 7.2 add_convert_fusion.3
  600.0 9.4 fusion.20
  609.5 4.2 gather_fusion.2
  613.6 4.6 reduce_sum.638
  618.3 13.4 %all-reduce.23 = (bf16[768]{0:T(1024)(128)(2,1)}, bf16[768]{0:T(1024)(128)(2,1)}, bf16[768]{0:T(1024)(128)(2,1)}, bf16[768]{0:T(1024)(128)(2,1)}, bf16[12]{0:T(2...) all-reduce(bf16[768]{0:T(1024)(128)(2,1)} %get-tuple-element.46, ...), channel_id=2, replica_groups=mesh['seq'=8,'grp'=4] {'grp'}, use_global_device_ids=true, to_apply=%region_32.33.clone | all-reduce | flops 22296 | bytes 89184
  658.2 4.0 select_convert_fusion
  665.4 368.4 %all-reduce.25 = (f32[192]{0:T(256)}, f32[192]{0:T(256)}, f32[192,2304]{1,0:T(8,128)}, f32[192]{0:T(256)}, f32[192]{0:T(256)}, /*index=5*/f32[16,12]{1,0:T(8,128...) all-reduce(f32[192]{0:T(256)S(1)} %dynamic-slice_convert_fusion.21,, ...), channel_id=1, replica_groups=mesh['seq'=8,'grp'=4] {'seq'}, use_global_device_ids=true, to_apply=%region_33.34 | all-reduce | flops 2365062 | bytes 14201520 | tf_op jit(solution)/shard_map/psum | solution.py:431
  (422 shorter events, 230.3 us)
Async XLA Ops:
  7.2 70.4 %copy-start = (bf16[768,2304]{1,0:T(8,128)(2,1)S(1)}, bf16[768,2304]{1,0:T(8,128)(2,1)}, u32[]{:S(2)}) copy-start(bf16[768,2304]{1,0:T(8,128)(2,1)} %param.46) | copy-start | bytes 10616836
  26.6 7.6 copy-start.97
  26.6 13.4 %copy-start.92 = (bf16[768]{0:T(1024)(128)(2,1)S(1)}, bf16[768]{0:T(1024)(128)(2,1)}, u32[]{:S(2)}) copy-start(bf16[768]{0:T(1024)(128)(2,1)} %param.44) | copy-start | bytes 4612
  26.6 13.4 %copy-start.93 = (bf16[768]{0:T(1024)(128)(2,1)S(1)}, bf16[768]{0:T(1024)(128)(2,1)}, u32[]{:S(2)}) copy-start(bf16[768]{0:T(1024)(128)(2,1)} %param.51) | copy-start | bytes 4612
  26.6 14.0 %copy-start.94 = (bf16[768]{0:T(1024)(128)(2,1)S(1)}, bf16[768]{0:T(1024)(128)(2,1)}, u32[]{:S(2)}) copy-start(bf16[768]{0:T(1024)(128)(2,1)} %param.55) | copy-start | bytes 4612
  26.6 77.4 %all-to-all-start.1 = ((bf16[16,112,768]{2,1,0:T(8,128)(2,1)}), bf16[16,112,768]{2,1,0:T(8,128)(2,1)}, u32[]{:S(2)}, u32[]{:S(2)}) async-start(bf16[16,112,768]{2,1,0:T(8,128)(2,1)} %bitcast.215), calls=%async_computation.1 | async-start | bytes 5505024 | tf_op jit(solution)/shard_map/all_to_all | solution.py:175
  39.3 19.8 %copy-start.52 = (f32[1,2,2,128]{3,1,2,0:T(2,128)}, f32[1,2,2,128]{3,1,2,0:T(2,128)S(1)}, u32[]{:S(2)}) copy-start(f32[1,2,2,128]{3,1,2,0:T(2,128)S(1)} %copy.283) | copy-start | bytes 6148
  39.9 36.1 %copy-start.37 = (f32[768]{0:T(1024)}, f32[768]{0:T(1024)S(1)}, u32[]{:S(2)}) copy-start(f32[768]{0:T(1024)S(1)} %convert_element_type.390) | copy-start | bytes 9220
  89.5 9.9 copy-start.56
  103.9 67.8 %all-to-all-start = ((bf16[16,112,768]{2,1,0:T(8,128)(2,1)}), bf16[16,112,768]{2,1,0:T(8,128)(2,1)}, u32[]{:S(2)}, u32[]{:S(2)}) async-start(bf16[16,112,768]{2,1,0:T(8,128)(2,1)} %bitcast.214), calls=%async_computation | async-start | bytes 5505024 | tf_op jit(solution)/shard_map/all_to_all | solution.py:176
  109.9 490.1 %reduce-scatter.11.cloned.1.call-start = ((), (), s32[]{:S(2)}) async-start(), calls=%async_computation.13 | async-start | bytes 20480 | tf_op jit(solution)/shard_map/reduce_scatter | solution.py:355
  121.7 5.3 copy-start.57
  127.1 4.9 copy-start.70
  127.1 4.9 copy-start.90
  127.1 4.9 copy-start.91
  127.1 4.9 copy-start.103
  133.8 7.2 copy-start.1
  195.8 11.1 %copy-start.13 = (bf16[2,896,12,64]{1,3,2,0:T(8,128)(2,1)S(1)}, bf16[2,896,12,64]{1,3,2,0:T(8,128)(2,1)}, u32[]{:S(2)}) copy-start(bf16[2,896,12,64]{1,3,2,0:T(8,128)(2,1)} %reshape.644) | copy-start | bytes 8257540
  195.8 11.1 %copy-start.85 = (f32[12]{0:T(128)S(1)}, f32[12]{0:T(128)}, u32[]{:S(2)}) copy-start(f32[12]{0:T(128)} %convert_element_type.411) | copy-start | bytes 148
  225.7 55.8 %copy-start.81 = (f32[512]{0:T(512)}, f32[512]{0:T(512)S(1)}, u32[]{:S(2)}) copy-start(f32[512]{0:T(512)S(1)} %rsqrt.63) | copy-start | bytes 6148
  229.0 47.8 %copy-start.17 = (f32[512,768]{1,0:T(8,128)}, f32[512,768]{1,0:T(8,128)S(1)}, u32[]{:S(2)}) copy-start(f32[512,768]{1,0:T(8,128)S(1)} %get-tuple-element.154) | copy-start | bytes 4718596
  229.0 47.7 %copy-start.46 = (f32[512]{0:T(512)}, f32[512]{0:T(512)S(1)}, u32[]{:S(2)}) copy-start(f32[512]{0:T(512)S(1)} %broadcast_multiply_fusion.1) | copy-start | bytes 6148
  229.4 47.4 %copy-start.76 = (f32[512]{0:T(512)}, f32[512]{0:T(512)S(1)}, u32[]{:S(2)}) copy-start(f32[512]{0:T(512)S(1)} %fusion.74) | copy-start | bytes 6148
  229.4 19.9 %copy-start.30 = (bf16[512,768]{1,0:T(8,128)(2,1)S(1)}, bf16[512,768]{1,0:T(8,128)(2,1)}, u32[]{:S(2)}) copy-start(bf16[512,768]{1,0:T(8,128)(2,1)} %fusion.50) | copy-start | bytes 2359300
  249.3 5.9 copy-start.40
  284.3 6.1 copy-start.86
  322.9 8.8 copy-start.2
  343.7 6.3 copy-start.83
  350.0 5.2 copy-start.33
  371.7 9.0 copy-start.61
  371.7 9.0 copy-start.65
  380.3 219.7 %reduce-scatter.19.cloned.1.call-start = ((), (), s32[]{:S(2)}) async-start(), calls=%async_computation.17 | async-start | bytes 1474560 | tf_op jit(solution)/shard_map/reduce_scatter | solution.py:400
  384.5 215.5 %reduce-scatter.15.cloned.1.call-start = ((), (), s32[]{:S(2)}) async-start(), calls=%async_computation.15 | async-start | bytes 1474560 | tf_op jit(solution)/shard_map/reduce_scatter | solution.py:379
  388.3 211.8 %reduce-scatter.13.cloned.1.call-start = ((), (), s32[]{:S(2)}) async-start(), calls=%async_computation.14 | async-start | bytes 1474560 | tf_op jit(solution)/shard_map/reduce_scatter | solution.py:367
  392.3 270.0 %reduce-scatter.9.cloned.1.call-start = ((), (), s32[]{:S(2)}) async-start(), calls=%async_computation.12 | async-start | bytes 4423680 | tf_op jit(solution)/shard_map/reduce_scatter | solution.py:346
  392.4 6.1 copy-start.14
  409.4 252.8 %reduce-scatter.23.cloned.1.call-start = ((), (), s32[]{:S(2)}) async-start(), calls=%async_computation.19 | async-start | bytes 5898240 | tf_op jit(solution)/shard_map/reduce_scatter | solution.py:424
  437.4 66.6 %all-to-all-start.3 = ((bf16[2,896,768]{2,0,1:T(2,128)(2,1)}), bf16[2,896,768]{2,0,1:T(2,128)(2,1)}, u32[]{:S(2)}, u32[]{:S(2)}) async-start(bf16[2,896,768]{2,0,1:T(2,128)(2,1)} %copy.272), calls=%async_computation.3 | async-start | bytes 5505024 | tf_op jit(solution)/shard_map/all_to_all | solution.py:275
  442.0 220.3 %reduce-scatter.21.cloned.1.call-start = ((), (), s32[]{:S(2)}) async-start(), calls=%async_computation.18 | async-start | bytes 5898240 | tf_op jit(solution)/shard_map/reduce_scatter | solution.py:412
  465.9 45.8 %copy-start.95 = (bf16[768]{0:T(1024)(128)(2,1)S(1)}, bf16[768]{0:T(1024)(128)(2,1)}, u32[]{:S(2)}) copy-start(bf16[768]{0:T(1024)(128)(2,1)} %param.73) | copy-start | bytes 4612
  465.9 47.6 %copy-start.72 = (f32[2,256]{1,0:T(2,128)S(1)}, f32[2,256]{1,0:T(2,128)}, u32[]{:S(2)}) copy-start(f32[2,256]{1,0:T(2,128)} %get-tuple-element.140) | copy-start | bytes 6148
  465.9 49.5 %copy-start.38 = (f32[768]{0:T(1024)S(1)}, f32[768]{0:T(1024)}, u32[]{:S(2)}) copy-start(f32[768]{0:T(1024)} %copy-done.37) | copy-start | bytes 9220
  465.9 49.5 %copy-start.41 = (f32[1,2,2,128]{3,1,2,0:T(2,128)S(1)}, f32[1,2,2,128]{3,1,2,0:T(2,128)}, u32[]{:S(2)}) copy-start(f32[1,2,2,128]{3,1,2,0:T(2,128)} %copy.282) | copy-start | bytes 6148
  504.0 66.2 %all-to-all-start.2 = ((bf16[2,896,768]{2,0,1:T(2,128)(2,1)}), bf16[2,896,768]{2,0,1:T(2,128)(2,1)}, u32[]{:S(2)}, u32[]{:S(2)}) async-start(bf16[2,896,768]{2,0,1:T(2,128)(2,1)} %copy.269), calls=%async_computation.2 | async-start | bytes 5505024 | tf_op jit(solution)/shard_map/all_to_all | solution.py:274
  508.4 157.0 %reduce-scatter.17.cloned.1.call-start = ((), (), s32[]{:S(2)}) async-start(), calls=%async_computation.16 | async-start | bytes 2949120 | tf_op jit(solution)/shard_map/reduce_scatter | solution.py:385
  515.4 4.8 copy-start.53
  515.4 4.8 copy-start.5
  515.4 4.8 copy-start.42
  (70 other events, 166.1 us)
Sparse Core Ops, SparseCore 0:
  380.4 18.3 reduce-scatter.10
  401.6 25.6 reduce-scatter.18
  429.9 25.7 reduce-scatter.14
  458.8 25.6 reduce-scatter.12
  486.9 40.4 reduce-scatter.8
  530.0 47.8 reduce-scatter.22
  580.4 48.4 reduce-scatter.20
  632.1 33.2 reduce-scatter.16
where the time goes:
time: 1050 us; the launch traced here: 1040 us
  blocking collectives  382 us (36%)
  matrix products  209 us (20%)
  local copies, waits for them, and re-layouts  155 us (15%)
  other arithmetic  155 us (15%)
  waiting for transfers between devices  99.5 us (9%)
  starting transfers between devices  23.5 us (2%)
  between operations  17.7 us (2%)
    psum x1, blocking collectives, local(): lax.psum((shares[0], shares[1], shares[2], shares[3], shares[4], shares[5...  368 us
    all_to_all x1, waiting for transfers between devices, local(): lax.all_to_all(keys_low, 'seq', split_axis=1, concat_axis=0, tiled=True)  44.1 us
    dot_general x7, matrix products, rows_dot(): return jnp.dot(left, right, preferred_element_type=jnp.float32)  41.8 us
    all_to_all x1, waiting for transfers between devices, local(): lax.all_to_all(values_low, 'seq', split_axis=1, concat_axis=0, tiled=True)  38.1 us
    dot_general x7, matrix products, left_dot(): lax.dot_general(left, right, (((0,), (0,)), ((), ())), preferred_element_...  35.9 us
    dot_general x7, matrix products, right_dot(): lax.dot_general(left, right, (((1,), (1,)), ((), ())), preferred_element_...  32.1 us
    unnamed x232, local copies, waits for them, and re-layouts  31 us
    convert_element_type x22, other arithmetic, local(): shares = (lax.psum_scatter(local_grads[0].astype(jnp.bfloat16), 'grp', sc...  26.5 us
  transfers between devices with their start and end apart: 12, of which 4 were waited for; matrix products, arithmetic and copies ran while one was open for 27% of the time, Pallas kernels for 0%

commit v1 on v0

v1 whole, which is shorter than its diff:
```python
import functools
import math

import jax
import jax.numpy as jnp
from jax import lax
from jax.experimental import pallas as pl
from jax.experimental.pallas import tpu as pltpu
from jax.sharding import PartitionSpec as P

H = 12
HD = 64
EPSILON = 1e-05
FACTOR = 1.0 / math.sqrt(HD)
MASKED = -1000000000.0
F32 = jnp.float32
BF16 = jnp.bfloat16
PAIR = 2 * HD
PAIRS = H // 2
VMEM_LIMIT = 60 * 1024 * 1024

(
    SELF_GAIN,
    SELF_SHIFT,
    SELF_QB,
    SELF_VB,
    SELF_HEAD,
    SELF_MIX_GAIN,
    SELF_MIX_SHIFT,
    SELF_OB,
    CROSS_GAIN,
    CROSS_SHIFT,
    CROSS_QB,
    CROSS_VB,
    CROSS_HEAD,
    CROSS_MIX_GAIN,
    CROSS_MIX_SHIFT,
    CROSS_OB,
    FFN_GAIN,
    FFN_SHIFT,
    FFN_OB,
) = range(19)


def dot(left, right):
    return jnp.dot(left, right, preferred_element_type=F32)


def dot_rows(left, right):
    return lax.dot_general(left, right, (((1,), (1,)), ((), ())), preferred_element_type=F32)


def dot_cols(left, right):
    return lax.dot_general(left, right, (((0,), (0,)), ((), ())), preferred_element_type=F32)


def normalize(values):
    average = jnp.mean(values, axis=-1, keepdims=True)
    centered = values - average
    spread = jnp.mean(centered * centered, axis=-1, keepdims=True)
    scale = lax.rsqrt(spread + EPSILON)
    return centered * scale, scale


def normalize_back(grad, normed, scale):
    mean_grad = jnp.mean(grad, axis=-1, keepdims=True)
    mean_both = jnp.mean(grad * normed, axis=-1, keepdims=True)
    return scale * (grad - mean_grad - normed * mean_both)


def total(values):
    return jnp.sum(values.astype(F32), axis=0, keepdims=True)


def lanes(start, size):
    return pl.ds(pl.multiple_of(start, 128), size)


def pick_head(values, half, axis):
    place = lax.broadcasted_iota(jnp.int32, values.shape, axis)
    inside = (place < HD) if half == 0 else (place >= HD)
    return jnp.where(inside, values, jnp.zeros_like(values))


def attend_pair(queries, keys, values, score_fn, e_ref, inv_ref, first):
    values_t = values.T
    parts = []
    for half in range(2):
        scores = score_fn(dot_rows(keys, pick_head(queries, half, 1)), first + half)
        peak = jnp.max(scores, axis=0, keepdims=True)
        weights = jnp.exp(scores - peak)
        inverse = 1.0 / jnp.sum(weights, axis=0, keepdims=True)
        low = weights.astype(BF16)
        e_ref[first + half] = low
        inv_ref[pl.ds(first + half, 1), :] = inverse
        parts.append(dot(values_t[half * HD : (half + 1) * HD], low) * inverse)
    return jnp.concatenate(parts, axis=0).T


def attend_pair_back(queries, keys, values, grad, prod, e_ref, inv_ref, first, keep_scores):
    keys_t = keys.T
    grad_t = grad.astype(F32).T
    prod_t = prod.T
    dq, dk, dv = [], None, None
    for half in range(2):
        rows = slice(half * HD, (half + 1) * HD)
        inverse = inv_ref[pl.ds(first + half, 1), :]
        delta = jnp.sum(prod_t[rows], axis=0, keepdims=True) * inverse
        grad_half = pick_head((grad_t * inverse).astype(BF16), half, 0)
        grad_probs = dot(values, grad_half)
        low = e_ref[first + half]
        grad_scores = (low.astype(F32) * (grad_probs - delta)).astype(BF16)
        if keep_scores is not None:
            keep_scores(grad_scores, first + half)
        dq.append(dot(keys_t[rows], grad_scores))
        part_k = dot(grad_scores, pick_head(queries, half, 1))
        part_v = dot_rows(low, grad_half)
        dk = part_k if dk is None else dk + part_k
        dv = part_v if dv is None else dv + part_v
    return jnp.concatenate(dq, axis=0).T * FACTOR, dk, dv


def self_forward_kernel(
    len_ref, prefix_ref, x_ref, bias_ref, qkv_w, out_w, q2_w, vec_ref,
    n1_ref, qkv_ref, e_ref, inv_ref, mixed_ref, z1_ref, x2_ref, n2_ref, q2_ref,
):
    item = pl.program_id(0)
    width = x_ref.shape[1]
    length = x_ref.shape[0]

    def vec(row):
        return vec_ref[row : row + 1, :]

    x = x_ref[...].astype(F32)
    normed, _ = normalize(x)
    n1_ref[...] = (normed * vec(SELF_GAIN) + vec(SELF_SHIFT)).astype(BF16)
    queries = dot(n1_ref[...], qkv_w[:, :width]) + vec(SELF_QB)
    qkv_ref[:, :width] = queries.astype(BF16) * jnp.asarray(FACTOR, BF16)
    qkv_ref[:, width : 2 * width] = dot(n1_ref[...], qkv_w[:, width : 2 * width]).astype(BF16)
    values = dot(n1_ref[...], qkv_w[:, 2 * width :]) + vec(SELF_VB)
    qkv_ref[:, 2 * width :] = values.astype(BF16)
    key_pos = lax.broadcasted_iota(jnp.int32, (length, length), 0)
    query_pos = lax.broadcasted_iota(jnp.int32, (length, length), 1)
    allowed = (key_pos < len_ref[item]) & ((key_pos <= query_pos) | (key_pos < prefix_ref[item]))
    inv_ref[...] = jnp.zeros_like(inv_ref)

    def scores_of(scores, head):
        return jnp.where(allowed, scores + bias_ref[head].astype(F32), MASKED)

    def one_pair(pair, _):
        base = pair * PAIR
        mixed_ref[:, lanes(base, PAIR)] = attend_pair(
            qkv_ref[:, lanes(base, PAIR)],
            qkv_ref[:, lanes(base + width, PAIR)],
            qkv_ref[:, lanes(base + 2 * width, PAIR)],
            scores_of, e_ref, inv_ref, 2 * pair,
        )
        return 0

    lax.fori_loop(0, PAIRS, one_pair, 0)
    normed, _ = normalize(mixed_ref[...] * vec(SELF_HEAD))
    z1_ref[...] = (normed * vec(SELF_MIX_GAIN) + vec(SELF_MIX_SHIFT)).astype(BF16)
    x2 = x + dot(z1_ref[...], out_w[...]) + vec(SELF_OB)
    x2_ref[...] = x2
    normed, _ = normalize(x2)
    n2_ref[...] = (normed * vec(CROSS_GAIN) + vec(CROSS_SHIFT)).astype(BF16)
    queries = dot(n2_ref[...], q2_w[...]) + vec(CROSS_QB)
    q2_ref[...] = queries.astype(BF16) * jnp.asarray(FACTOR, BF16)


def gelu_parts(hidden):
    gate = 0.5 * (1.0 + lax.erf(hidden * math.sqrt(0.5)))
    slope = hidden * (jnp.exp(-0.5 * hidden * hidden) * (1.0 / math.sqrt(2.0 * math.pi)))
    return hidden * gate, gate + slope


def cross_forward_kernel(
    item, count, mem_len_ref, dec_len_ref, x2_ref, q2_ref, mem_ref, cot_ref,
    kv_w, out_w, in_w, ffn_w, vec_ref, wide_ref, *rest,
):
    outs = rest[len(rest) - count - 2 :]
    (
        out_ref, kv_ref, e_ref, inv_ref, mixed_ref, z2_ref, n3_ref, hid_ref, mid_ref,
        cot_low_ref, gx3_ref, branch_ref, vg_ref, wg_ref,
    ) = outs[:count]
    act_ref, slope_ref = outs[count:]
    width = x2_ref.shape[1]
    length = x2_ref.shape[0]
    mem_tokens = mem_ref.shape[0]
    ff = in_w.shape[1]
    tiles = ff // width

    def vec(row):
        return vec_ref[row : row + 1, :]

    kv_ref[:, :width] = dot(mem_ref[...], kv_w[:, :width]).astype(BF16)
    kv_ref[:, width:] = (dot(mem_ref[...], kv_w[:, width:]) + vec(CROSS_VB)).astype(BF16)
    mem_len = mem_len_ref[item]
    inv_ref[...] = jnp.zeros_like(inv_ref)

    def scores_of(scores, head):
        del head
        key_pos = lax.broadcasted_iota(jnp.int32, (mem_tokens, length), 0)
        return jnp.where(key_pos < mem_len, scores, MASKED)

    def one_pair(pair, _):
        base = pair * PAIR
        mixed_ref[:, lanes(base, PAIR)] = attend_pair(
            q2_ref[:, lanes(base, PAIR)],
            kv_ref[:, lanes(base, PAIR)],
            kv_ref[:, lanes(base + width, PAIR)],
            scores_of, e_ref, inv_ref, 2 * pair,
        )
        return 0

    lax.fori_loop(0, PAIRS, one_pair, 0)
    normed, _ = normalize(mixed_ref[...] * vec(CROSS_HEAD))
    z2_ref[...] = (normed * vec(CROSS_MIX_GAIN) + vec(CROSS_MIX_SHIFT)).astype(BF16)
    x3 = x2_ref[...] + dot(z2_ref[...], out_w[...]) + vec(CROSS_OB)
    norm3, scale3 = normalize(x3)
    n3_ref[...] = (norm3 * vec(FFN_GAIN) + vec(FFN_SHIFT)).astype(BF16)

    def hidden_tile(tile, sums):
        cols = lanes(tile * width, width)
        hidden = dot(n3_ref[...], in_w[:, cols]) + wide_ref[0:1, cols]
        act, slope = gelu_parts(hidden)
        act_ref[:, cols] = act
        slope_ref[:, cols] = slope
        return sums + jnp.sum(act, axis=-1, keepdims=True)

    sums = lax.fori_loop(0, tiles, hidden_tile, jnp.zeros((length, 1), F32))
    average = sums / ff

    def spread_tile(tile, sums):
        centered = act_ref[:, lanes(tile * width, width)] - average
        return sums + jnp.sum(centered * centered, axis=-1, keepdims=True)

    sums = lax.fori_loop(0, tiles, spread_tile, jnp.zeros((length, 1), F32))
    scale = lax.rsqrt(sums / ff + EPSILON)

    def middle_tile(tile, _):
        cols = lanes(tile * width, width)
        normed = (act_ref[:, cols] - average) * scale
        act_ref[:, cols] = normed
        mid_ref[:, cols] = (normed * wide_ref[1:2, cols] + wide_ref[2:3, cols]).astype(BF16)
        return 0

    lax.fori_loop(0, tiles, middle_tile, 0)
    result = x3 + dot(mid_ref[...], ffn_w[...]) + vec(FFN_OB)
    out_ref[...] = result.astype(BF16)

    valid = lax.broadcasted_iota(jnp.int32, (length, 1), 0) < dec_len_ref[item]
    cot = jnp.where(valid, cot_ref[...].astype(F32), 0.0)
    cot_low_ref[...] = cot.astype(BF16)
    wg_ref[...] = jnp.zeros_like(wg_ref)
    vg_ref[...] = jnp.zeros_like(vg_ref)

    def grad_mid_tile(tile, sums):
        cols = lanes(tile * width, width)
        grad_mid = dot_rows(cot_low_ref[...], ffn_w[cols, :])
        normed = act_ref[:, cols]
        wg_ref[1:2, cols] = total(grad_mid * normed)
        wg_ref[2:3, cols] = total(grad_mid)
        grad = grad_mid * wide_ref[1:2, cols]
        hid_ref[:, cols] = grad.astype(BF16)
        return (
            sums[0] + jnp.sum(grad, axis=-1, keepdims=True),
            sums[1] + jnp.sum(grad * normed, axis=-1, keepdims=True),
        )

    zero = jnp.zeros((length, 1), F32)
    sum_grad, sum_both = lax.fori_loop(0, tiles, grad_mid_tile, (zero, zero))
    mean_grad, mean_both = sum_grad / ff, sum_both / ff

    def hidden_back_tile(tile, _):
        cols = lanes(tile * width, width)
        grad = dot_rows(cot_low_ref[...], ffn_w[cols, :]) * wide_ref[1:2, cols]
        grad = scale * (grad - mean_grad - act_ref[:, cols] * mean_both)
        low = (grad * slope_ref[:, cols]).astype(BF16)
        hid_ref[:, cols] = low
        wg_ref[0:1, cols] = total(low)
        return 0

    lax.fori_loop(0, tiles, hidden_back_tile, 0)
    grad_n3 = dot_rows(hid_ref[...], in_w[...])
    vg_ref[FFN_GAIN : FFN_GAIN + 1, :] = total(grad_n3 * norm3)
    vg_ref[FFN_SHIFT : FFN_SHIFT + 1, :] = total(grad_n3)
    vg_ref[FFN_OB : FFN_OB + 1, :] = total(cot_low_ref[...])
    gx3 = normalize_back(grad_n3 * vec(FFN_GAIN), norm3, scale3) + cot
    gx3_ref[...] = gx3
    branch_ref[...] = gx3.astype(BF16)
    vg_ref[CROSS_OB : CROSS_OB + 1, :] = total(branch_ref[...])


def cross_back_kernel(
    item, count, branch_ref, gx3_ref, mixed_ref, kv_ref, e_ref, inv_ref, q2_ref, x2_ref,
    kv_w, out_w, q2_w, vec_ref, *rest,
):
    del item
    outs = rest[len(rest) - count - 2 :]
    dq_ref, dkv_ref, gmem_ref, gx2_ref, branch2_ref, vg_ref = outs[:count]
    grad_ref, prod_ref = outs[count:]
    width = x2_ref.shape[1]

    def vec(row):
        return vec_ref[row : row + 1, :]

    def put(row, value):
        vg_ref[row : row + 1, :] = value

    vg_ref[...] = jnp.zeros_like(vg_ref)
    mixed = mixed_ref[...]
    normed, scale = normalize(mixed * vec(CROSS_HEAD))
    grad = dot_rows(branch_ref[...], out_w[...])
    put(CROSS_MIX_GAIN, total(grad * normed))
    put(CROSS_MIX_SHIFT, total(grad))
    grad = normalize_back(grad * vec(CROSS_MIX_GAIN), normed, scale)
    put(CROSS_HEAD, total(grad * mixed))
    grad = (grad * vec(CROSS_HEAD)).astype(BF16)
    grad_ref[...] = grad
    prod_ref[...] = grad.astype(F32) * mixed

    def one_pair(pair, _):
        base = pair * PAIR
        cols = lanes(base, PAIR)
        dq, dk, dv = attend_pair_back(
            q2_ref[:, cols], kv_ref[:, cols], kv_ref[:, lanes(base + width, PAIR)],
            grad_ref[:, cols], prod_ref[:, cols], e_ref, inv_ref, 2 * pair, None,
        )
        dq_ref[:, cols] = dq.astype(BF16)
        dkv_ref[:, cols] = dk.astype(BF16)
        dkv_ref[:, lanes(base + width, PAIR)] = dv.astype(BF16)
        return 0

    lax.fori_loop(0, PAIRS, one_pair, 0)
    put(CROSS_VB, total(dkv_ref[:, width:]))
    step = 256

    def memory_tile(tile, _):
        cols = lanes(tile * step, step)
        gmem_ref[:, cols] = dot_rows(dkv_ref[...], kv_w[cols, :]).astype(BF16)
        return 0

    lax.fori_loop(0, width // step, memory_tile, 0)
    put(CROSS_QB, total(dq_ref[...]))
    normed, scale = normalize(x2_ref[...])
    grad = dot_rows(dq_ref[...], q2_w[...])
    put(CROSS_GAIN, total(grad * normed))
    put(CROSS_SHIFT, total(grad))
    gx2 = normalize_back(grad * vec(CROSS_GAIN), normed, scale) + gx3_ref[...]
    gx2_ref[...] = gx2
    branch2_ref[...] = gx2.astype(BF16)
    put(SELF_OB, total(branch2_ref[...]))


def self_back_kernel(
    branch_ref, gx2_ref, mixed_ref, qkv_ref, e_ref, inv_ref, x_ref, qkv_w, out_w, vec_ref,
    dqkv_ref, gx_ref, vg_ref, diag_ref, grad_ref, prod_ref,
):
    width = x_ref.shape[1]
    length = x_ref.shape[0]

    def vec(row):
        return vec_ref[row : row + 1, :]

    def put(row, value):
        vg_ref[row : row + 1, :] = value

    vg_ref[...] = jnp.zeros_like(vg_ref)
    diag_ref[...] = jnp.zeros_like(diag_ref)
    mixed = mixed_ref[...]
    normed, scale = normalize(mixed * vec(SELF_HEAD))
    grad = dot_rows(branch_ref[...], out_w[...])
    put(SELF_MIX_GAIN, total(grad * normed))
    put(SELF_MIX_SHIFT, total(grad))
    grad = normalize_back(grad * vec(SELF_MIX_GAIN), normed, scale)
    put(SELF_HEAD, total(grad * mixed))
    grad = (grad * vec(SELF_HEAD)).astype(BF16)
    grad_ref[...] = grad
    prod_ref[...] = grad.astype(F32) * mixed

    backwards = (
        lax.broadcasted_iota(jnp.int32, (length, length), 0)
        + lax.broadcasted_iota(jnp.int32, (length, length), 1)
        == length - 1
    ).astype(F32).astype(BF16)

    def keep_scores(scores, head):
        flipped = dot(backwards, scores)
        padded = jnp.concatenate([flipped, jnp.zeros_like(flipped)], axis=1)
        rolled = pltpu.roll(padded, 0, 1, stride=1, stride_axis=0)
        diag_ref[pl.ds(head, 1), :] = jnp.sum(rolled, axis=0, keepdims=True)

    def one_pair(pair, _):
        base = pair * PAIR
        cols = lanes(base, PAIR)
        dq, dk, dv = attend_pair_back(
            qkv_ref[:, cols], qkv_ref[:, lanes(base + width, PAIR)],
            qkv_ref[:, lanes(base + 2 * width, PAIR)],
            grad_ref[:, cols], prod_ref[:, cols], e_ref, inv_ref, 2 * pair, keep_scores,
        )
        dqkv_ref[:, cols] = dq.astype(BF16)
        dqkv_ref[:, lanes(base + width, PAIR)] = dk.astype(BF16)
        dqkv_ref[:, lanes(base + 2 * width, PAIR)] = dv.astype(BF16)
        return 0

    lax.fori_loop(0, PAIRS, one_pair, 0)
    put(SELF_QB, total(dqkv_ref[:, :width]))
    put(SELF_VB, total(dqkv_ref[:, 2 * width :]))
    normed, scale = normalize(x_ref[...].astype(F32))
    grad = dot_rows(dqkv_ref[...], qkv_w[...])
    put(SELF_GAIN, total(grad * normed))
    put(SELF_SHIFT, total(grad))
    gx = normalize_back(grad * vec(SELF_GAIN), normed, scale) + gx2_ref[...]
    gx_ref[...] = gx.astype(BF16)


def per_item(shape):
    return pl.BlockSpec((None,) + shape, lambda i: (i,) + (0,) * len(shape))


def whole(array):
    return pl.BlockSpec(array.shape, lambda i: (0,) * array.ndim)


def at_item(array, item):
    return pl.BlockSpec((None,) + array.shape[1:], lambda i: (item,) + (0,) * (array.ndim - 1))


SMEM = pl.BlockSpec(memory_space=pltpu.SMEM)


def item_call(kernel, name, item, items, ins, in_specs, out_shapes, scratch, before, flops):
    shapes = [jax.ShapeDtypeStruct((items,) + s, d) for s, d in out_shapes]
    specs = [at_item(s, item) for s in shapes]
    aliases = {}
    if before is not None:
        aliases = {len(ins) + i: i for i in range(len(shapes))}
        ins = tuple(ins) + tuple(before)
        in_specs = list(in_specs) + [pl.BlockSpec(memory_space=pl.ANY)] * len(shapes)
    return pl.pallas_call(
        functools.partial(kernel, item, len(shapes)),
        out_shape=shapes,
        grid=(1,),
        in_specs=in_specs,
        out_specs=specs,
        scratch_shapes=scratch,
        input_output_aliases=aliases,
        compiler_params=pltpu.CompilerParams(vmem_limit_bytes=VMEM_LIMIT),
        cost_estimate=pl.CostEstimate(flops=flops, bytes_accessed=30_000_000, transcendentals=0),
        name=name,
    )(*ins)


def self_forward(dec_len, prefix, x, bias, qkv_w, out_w, q2_w, vecs):
    items, length, width = x.shape
    outs = [
        ((length, width), BF16),
        ((length, 3 * width), BF16),
        ((H, length, length), BF16),
        ((16, length), F32),
        ((length, width), F32),
        ((length, width), BF16),
        ((length, width), F32),
        ((length, width), BF16),
        ((length, width), BF16),
    ]
    return pl.pallas_call(
        self_forward_kernel,
        out_shape=[jax.ShapeDtypeStruct((items,) + s, d) for s, d in outs],
        grid=(items,),
        in_specs=[SMEM, SMEM, per_item((length, width))]
        + [whole(a) for a in (bias, qkv_w, out_w, q2_w, vecs)],
        out_specs=[per_item(s) for s, _ in outs],
        compiler_params=pltpu.CompilerParams(vmem_limit_bytes=VMEM_LIMIT),
        cost_estimate=pl.CostEstimate(
            flops=items * 2 * length * width * 8 * width, bytes_accessed=30_000_000, transcendentals=0
        ),
        name="self_forward",
    )(dec_len, prefix, x, bias, qkv_w, out_w, q2_w, vecs)


def cross_forward(item, before, mem_len, dec_len, x2, q2, mem, cot, kv_w, out_w, in_w, ffn_w, vecs, wides):
    items, length, width = x2.shape
    mem_tokens = mem.shape[0]
    ff = in_w.shape[1]
    outs = [
        ((length, width), BF16),
        ((mem_tokens, 2 * width), BF16),
        ((H, mem_tokens, length), BF16),
        ((16, length), F32),
        ((length, width), F32),
        ((length, width), BF16),
        ((length, width), BF16),
        ((length, ff), BF16),
        ((length, ff), BF16),
        ((length, width), BF16),
        ((length, width), F32),
        ((length, width), BF16),
        (vecs.shape, F32),
        (wides.shape, F32),
    ]
    ins = (mem_len, dec_len, x2, q2, mem, cot, kv_w, out_w, in_w, ffn_w, vecs, wides)
    specs = [SMEM, SMEM, at_item(x2, item), at_item(q2, item), whole(mem), at_item(cot, item)]
    specs += [whole(a) for a in (kv_w, out_w, in_w, ffn_w, vecs, wides)]
    scratch = [pltpu.VMEM((length, ff), F32), pltpu.VMEM((length, ff), F32)]
    flops = 2 * length * width * (5 * ff + width) + 4 * mem_tokens * width * (width + 4 * length)
    return item_call(
        cross_forward_kernel, "cross_forward", item, items, ins, specs, outs, scratch, before, flops
    )


def cross_back(item, before, branch, gx3, mixed, kv, e, inv, q2, x2, kv_w, out_w, q2_w, vecs):
    items, length, width = x2.shape
    mem_tokens = kv.shape[1]
    outs = [
        ((length, width), BF16),
        ((mem_tokens, 2 * width), BF16),
        ((mem_tokens, width), BF16),
        ((length, width), F32),
        ((length, width), BF16),
        (vecs.shape, F32),
    ]
    stacked = (branch, gx3, mixed, kv, e, inv, q2, x2)
    ins = stacked + (kv_w, out_w, q2_w, vecs)
    specs = [at_item(a, item) for a in stacked] + [whole(a) for a in (kv_w, out_w, q2_w, vecs)]
    scratch = [pltpu.VMEM((length, width), BF16), pltpu.VMEM((length, width), F32)]
    flops = 2 * length * width * 2 * width + 4 * mem_tokens * width * (width + 8 * length)
    return item_call(
        cross_back_kernel, "cross_back", item, items, ins, specs, outs, scratch, before, flops
    )


def self_back(branch, gx2, mixed, qkv, e, inv, x, qkv_w, out_w, vecs):
    items, length, width = x.shape
    outs = [
        ((length, 3 * width), BF16),
        ((length, width), BF16),
        (vecs.shape, F32),
        ((16, 2 * length), F32),
    ]
    stacked = (branch, gx2, mixed, qkv, e, inv, x)
    return pl.pallas_call(
        self_back_kernel,
        out_shape=[jax.ShapeDtypeStruct((items,) + s, d) for s, d in outs],
        grid=(items,),
        in_specs=[per_item(a.shape[1:]) for a in stacked] + [whole(a) for a in (qkv_w, out_w, vecs)],
        out_specs=[per_item(s) for s, _ in outs],
        scratch_shapes=[pltpu.VMEM((length, width), BF16), pltpu.VMEM((length, width), F32)],
        compiler_params=pltpu.CompilerParams(vmem_limit_bytes=VMEM_LIMIT),
        cost_estimate=pl.CostEstimate(
            flops=items * 2 * length * width * 8 * width, bytes_accessed=30_000_000, transcendentals=0
        ),
        name="self_back",
    )(*stacked, qkv_w, out_w, vecs)


def rel_bias_of(table, length):
    count = table.shape[0]
    positions = jnp.arange(length, dtype=jnp.int32)
    offset = jnp.clip(positions[:, None] - positions[None, :], -(count // 2), count // 2 - 1)
    one_hot = (offset + count // 2)[None] == jnp.arange(count, dtype=jnp.int32)[:, None, None]
    return lax.dot_general(
        table, one_hot.astype(BF16), (((0,), (0,)), ((), ())), preferred_element_type=F32
    ).astype(BF16)


def table_grad(diag, count):
    length = diag.shape[1] // 2
    offset = length - 1 - jnp.arange(2 * length, dtype=jnp.int32)
    bucket = jnp.clip(offset, -(count // 2), count // 2 - 1) + count // 2
    one_hot = (bucket[:, None] == jnp.arange(count, dtype=jnp.int32)[None, :]).astype(F32)
    return jnp.dot(diag, one_hot, precision=lax.Precision.HIGHEST).T


def reduce_plain(grads):
    shares = [
        lax.psum_scatter(g, "grp", scatter_dimension=0, tiled=True).astype(F32) for g in grads
    ]
    return lax.psum(tuple(shares), "seq")


CORE_PAIRS = [(0, 1), (1, 0), (2, 3), (3, 2)]
Y_PAIRS = [(0, 2), (2, 0), (1, 3), (3, 1)]
X_PAIRS = [(0, 1), (1, 0), (2, 3), (3, 2), (4, 5), (5, 4), (6, 7), (7, 6)]
Z_IN = [(0, 2), (1, 3), (6, 4), (7, 5)]
Z_MID = [(2, 4), (4, 2), (3, 5), (5, 3)]
Z_OUT = [(2, 0), (3, 1), (4, 6), (5, 7)]


def add_low(left, right):
    return (left.astype(F32) + right.astype(F32)).astype(BF16)


def take_at(array, index, axis):
    return lax.dynamic_index_in_dim(array, index, axis, keepdims=False)


def reduce_pairs(local):
    group = lax.axis_index("grp")
    seq = lax.axis_index("seq")
    core, y = group % 2, group // 2
    x, z = seq % 2, seq // 2
    rows = local.shape[0]
    parts = local.reshape((2, 2, rows // 4) + local.shape[1:])
    got = lax.ppermute(take_at(parts, 1 - core, 1), "grp", CORE_PAIRS)
    mine = add_low(take_at(parts, core, 1), got)
    got = lax.ppermute(take_at(mine, 1 - y, 0), "grp", Y_PAIRS)
    mine = add_low(take_at(mine, y, 0), got)
    mine = mine.reshape((2, rows // 8) + local.shape[1:])
    got = lax.ppermute(take_at(mine, 1 - x, 0), "seq", X_PAIRS)
    mine = add_low(take_at(mine, x, 0), got)
    got = lax.ppermute(mine, "seq", Z_IN)
    mine = add_low(mine, got)
    got = lax.ppermute(mine, "seq", Z_MID)
    mine = add_low(mine, got)
    got = lax.ppermute(mine, "seq", Z_OUT)
    inner = (z == 1) | (z == 2)
    mine = jnp.where(inner, mine, got)
    got = lax.ppermute(mine, "seq", X_PAIRS)
    first = jnp.where(x == 0, mine, got)
    second = jnp.where(x == 0, got, mine)
    return jnp.concatenate([first, second], axis=0).astype(F32)


def quarter_rows(vector):
    return vector.reshape(4, -1)


def local(
    dec_in,
    memory,
    cotangent,
    dec_len,
    task_prefix,
    owner,
    mem_len,
    self_norm_gain,
    self_norm_shift,
    self_qkv,
    self_q_bias,
    self_v_bias,
    rel_bias_table,
    self_head_gain,
    self_mix_gain,
    self_mix_shift,
    self_out,
    self_out_bias,
    cross_norm_gain,
    cross_norm_shift,
    cross_q,
    cross_q_bias,
    cross_kv,
    cross_v_bias,
    cross_head_gain,
    cross_mix_gain,
    cross_mix_shift,
    cross_out,
    cross_out_bias,
    ffn_norm_gain,
    ffn_norm_shift,
    ffn_in,
    ffn_in_bias,
    ffn_mid_gain,
    ffn_mid_shift,
    ffn_out,
    ffn_out_bias,
):
    items, length, width = dec_in.shape
    rows = items * length
    items_grp = owner.shape[1]
    shard_tokens = memory.shape[1]
    seq_size = lax.axis_size("seq")
    grp_size = lax.axis_size("grp")
    mem_tokens = shard_tokens * seq_size
    group = lax.axis_index("grp")
    seq_index = lax.axis_index("seq")
    paired = seq_size == 8 and grp_size == 4

    owner_row = lax.dynamic_index_in_dim(owner, group, 0, keepdims=False)
    inverse = (
        jnp.zeros((items_grp,), jnp.int32).at[owner_row].set(jnp.arange(items_grp, dtype=jnp.int32))
    )
    mine = lax.dynamic_slice_in_dim(inverse, seq_index * items, items)
    my_mem_len = jnp.take(mem_len, group * items_grp + mine)

    memories = []
    for item in range(items):
        sent = jnp.take(memory, inverse.reshape(seq_size, items)[:, item], axis=0)
        got = lax.all_to_all(sent, "seq", split_axis=0, concat_axis=0, tiled=True)
        memories.append(got.reshape(mem_tokens, width))

    def spread(gain):
        return jnp.repeat(gain, HD)

    vectors = [
        self_norm_gain, self_norm_shift, self_q_bias, self_v_bias, spread(self_head_gain),
        self_mix_gain, self_mix_shift, self_out_bias, cross_norm_gain, cross_norm_shift,
        cross_q_bias, cross_v_bias, spread(cross_head_gain), cross_mix_gain, cross_mix_shift,
        cross_out_bias, ffn_norm_gain, ffn_norm_shift, ffn_out_bias,
    ]
    vecs = jnp.stack(vectors + [jnp.zeros_like(self_norm_gain)] * 5).astype(F32)
    wides = jnp.stack([ffn_in_bias, ffn_mid_gain, ffn_mid_shift] + [jnp.zeros_like(ffn_in_bias)] * 5)
    wides = wides.astype(F32)
    bias = rel_bias_of(rel_bias_table, length)

    n1, qkv, e1, inv1, mixed1, z1, x2, n2, q2 = self_forward(
        dec_len, task_prefix, dec_in, bias, self_qkv, self_out, cross_q, vecs
    )

    ahead, back = None, None
    returned = []
    for item in range(items):
        ahead = cross_forward(
            item, ahead, my_mem_len, dec_len, x2, q2, memories[item], cotangent,
            cross_kv, cross_out, ffn_in, ffn_out, vecs, wides,
        )
        (out, kv, e2, inv2, mixed2, z2, n3, hid, mid, cot_low, gx3, branch3, vg2, wg2) = ahead
        back = cross_back(
            item, back, branch3, gx3, mixed2, kv, e2, inv2, q2, x2,
            cross_kv, cross_out, cross_q, vecs,
        )
        dq2, dkv, gmem, gx2, branch2, vg3 = back
        sent = gmem[item].reshape(seq_size, shard_tokens, width)
        returned.append(
            lax.all_to_all(sent, "seq", split_axis=0, concat_axis=0, tiled=True)
        )
    dqkv, gx, vg4, diag = self_back(
        branch2, gx2, mixed1, qkv, e1, inv1, dec_in, self_qkv, self_out, vecs
    )

    by_slot = jnp.stack(returned, axis=1).reshape(items_grp, shard_tokens, width)
    grad_memory = jnp.take(by_slot, owner_row, axis=0)

    def weight_grad(left, right):
        return dot_cols(left.reshape(-1, left.shape[-1]), right.reshape(-1, right.shape[-1])).astype(BF16)

    grad_ffn_out = weight_grad(mid, cot_low)
    grad_ffn_in = weight_grad(n3, hid)
    grad_cross_out = weight_grad(z2, branch3)
    grad_cross_kv = sum(dot_cols(memories[i], dkv[i]) for i in range(items)).astype(BF16)
    grad_cross_q = weight_grad(n2, dq2)
    grad_self_out = weight_grad(z1, branch2)
    grad_self_qkv = weight_grad(n1, dqkv)

    vg = jnp.sum(vg2 + vg3 + vg4, axis=0)
    wg = jnp.sum(wg2, axis=0)
    heads_self = jnp.sum(vg[SELF_HEAD].reshape(H, HD), axis=1)
    heads_cross = jnp.sum(vg[CROSS_HEAD].reshape(H, HD), axis=1)
    grad_table = table_grad(jnp.sum(diag, axis=0)[:H], rel_bias_table.shape[0])

    pieces = [vg[row] for row in range(19) if row not in (SELF_HEAD, CROSS_HEAD)]
    pieces += [wg[0], wg[1], wg[2], grad_table.reshape(-1), heads_self, heads_cross]
    sizes = [p.size // grp_size for p in pieces]
    small = jnp.concatenate([p.reshape(grp_size, -1) for p in pieces], axis=1)
    small = jnp.pad(small, ((0, 0), (0, -small.shape[1] % 128)))

    big = [
        grad_ffn_out, grad_ffn_in, grad_cross_out, grad_cross_kv, grad_cross_q, grad_self_out,
        grad_self_qkv,
    ]
    if paired:
        big = [reduce_pairs(g) for g in big]
    else:
        big = reduce_plain(big)
    small = lax.psum(lax.psum_scatter(small, "grp", scatter_dimension=0, tiled=True), "seq")[0]

    ends = [sum(sizes[: i + 1]) for i in range(len(sizes))]
    small = [small[end - size : end] for end, size in zip(ends, sizes)]
    (
        g_self_norm_gain, g_self_norm_shift, g_self_q_bias, g_self_v_bias, g_self_mix_gain,
        g_self_mix_shift, g_self_out_bias, g_cross_norm_gain, g_cross_norm_shift, g_cross_q_bias,
        g_cross_v_bias, g_cross_mix_gain, g_cross_mix_shift, g_cross_out_bias, g_ffn_norm_gain,
        g_ffn_norm_shift, g_ffn_out_bias, g_ffn_in_bias, g_ffn_mid_gain, g_ffn_mid_shift, g_table,
        g_self_head, g_cross_head,
    ) = small
    g_ffn_out, g_ffn_in, g_cross_out, g_cross_kv, g_cross_q, g_self_out, g_self_qkv = big
    return (
        out,
        gx,
        grad_memory,
        g_self_norm_gain,
        g_self_norm_shift,
        g_self_qkv,
        g_self_q_bias,
        g_self_v_bias,
        g_table.reshape(-1, H),
        g_self_head,
        g_self_mix_gain,
        g_self_mix_shift,
        g_self_out,
        g_self_out_bias,
        g_cross_norm_gain,
        g_cross_norm_shift,
        g_cross_q,
        g_cross_q_bias,
        g_cross_kv,
        g_cross_v_bias,
        g_cross_head,
        g_cross_mix_gain,
        g_cross_mix_shift,
        g_cross_out,
        g_cross_out_bias,
        g_ffn_norm_gain,
        g_ffn_norm_shift,
        g_ffn_in,
        g_ffn_in_bias,
        g_ffn_mid_gain,
        g_ffn_mid_shift,
        g_ffn_out,
        g_ffn_out_bias,
    )


def solution(mesh):
    rows = P(("seq", "grp"), None, None)
    matrix, vector = P("grp", None), P("grp")
    in_specs = (rows, P("grp", "seq", None), rows, P(("seq", "grp")), P(("seq", "grp"))) + (P(),) * 32
    out_specs = (
        rows, rows, P("grp", "seq", None),
        vector, vector, matrix, vector, vector, matrix, vector, vector, vector, matrix, vector,
        vector, vector, matrix, vector, matrix, vector, vector, vector, vector, matrix, vector,
        vector, vector, matrix, vector, vector, vector, matrix, vector,
    )
    return jax.shard_map(local, mesh=mesh, in_specs=in_specs, out_specs=out_specs, check_vma=False)
```

time: 1050 us -> 622 us (0.59)
  blocking collectives: 382 us -> 37.1 us
  matrix products: 209 us -> 28.9 us
  Pallas kernels: 0 us -> 152 us
  other arithmetic: 155 us -> 44.2 us
  waiting for transfers between devices: 99.5 us -> 191 us
  local copies, waits for them, and re-layouts: 155 us -> 68.6 us
  starting transfers between devices: 23.5 us -> 77.6 us
    psum x1, blocking collectives: 368 us -> 37.1 us  [local(): lax.psum(lax.psum_scatter(small, 'grp', scatter_dimension=0, tiled=True),...]
    dot_general x35 -> x10, matrix products: 209 us -> 28.9 us  [the longest x8 22.7 us: dot_cols(): lax.dot_general(left, right, (((0,), (0,)), ((), ())), preferred_element_...]
    pallas_call x0 -> x6, Pallas kernels: none -> 152 us  [the longest x4 111 us: item_call(): pl.pallas_call(functools.partial(kernel, item, len(shapes)), out_shape=sh...]
    ppermute x0 -> x49, waiting for transfers between devices: none -> 140 us  [the longest x7 50.9 us: reduce_pairs(): got = lax.ppermute(mine, 'seq', Z_OUT)]
    all_to_all x4, waiting for transfers between devices: 96.2 us -> 26.8 us  [the longest x2 21.7 us: local(): got = lax.all_to_all(sent, 'seq', split_axis=0, concat_axis=0, tiled=True)]
    ppermute x0 -> x49, starting transfers between devices: none -> 56 us  [the longest x7 25.9 us: reduce_pairs(): got = lax.ppermute(mine, 'seq', Z_IN)]
    convert_element_type x52 -> x44, other arithmetic: 83.5 us -> 27.6 us  [the longest x35 18.1 us: add_low(): return (left.astype(F32) + right.astype(F32)).astype(BF16)]
    reduce_sum x24 -> x5, other arithmetic: 58.2 us -> 2.38 us  [the longest x1 1.46 us: local(): grad_table = table_grad(jnp.sum(diag, axis=0)[:H], rel_bias_table.shape[0])]
  transfers between devices with their start and end apart: 12 -> 54, of which waited for: 4 -> 31; matrix products, arithmetic and copies ran while one was open for 27% -> 19% of each run, Pallas kernels for 0% -> 19%
where the time goes in v1:
time: 622 us; the launch traced here: 615 us
  waiting for transfers between devices  191 us (31%)
  Pallas kernels  152 us (24%)
  starting transfers between devices  77.6 us (12%)
  local copies, waits for them, and re-layouts  68.6 us (11%)
  other arithmetic  44.2 us (7%)
  blocking collectives  37.1 us (6%)
  matrix products  28.9 us (5%)
  between operations  16 us (3%)
    pallas_call x4, Pallas kernels, item_call(): pl.pallas_call(functools.partial(kernel, item, len(shapes)), out_shape=sh...  111 us
    ppermute x7, waiting for transfers between devices, reduce_pairs(): got = lax.ppermute(mine, 'seq', Z_OUT)  50.9 us
    psum x1, blocking collectives, local(): lax.psum(lax.psum_scatter(small, 'grp', scatter_dimension=0, tiled=True),...  37.1 us
    ppermute x7, waiting for transfers between devices, reduce_pairs(): got = lax.ppermute(mine, 'seq', X_PAIRS)  34.4 us
    ppermute x7, starting transfers between devices, reduce_pairs(): got = lax.ppermute(mine, 'seq', Z_IN)  25.9 us
    ppermute x7, waiting for transfers between devices, reduce_pairs(): got = lax.ppermute(take_at(mine, 1 - x, 0), 'seq', X_PAIRS)  24.3 us
    unnamed x2, waiting for transfers between devices  23.6 us
    dot_general x8, matrix products, dot_cols(): lax.dot_general(left, right, (((0,), (0,)), ((), ())), preferred_element_...  22.7 us
  transfers between devices with their start and end apart: 54, of which 31 were waited for; matrix products, arithmetic and copies ran while one was open for 19% of the time, Pallas kernels for 19%

profile of v1, /device:TPU:0, one launch (start us, length us, event | category | flops | bytes accessed | tf_op | source)
XLA Modules:
  0.0 614.9 jit_solution(2072381895140073739)
XLA Ops:
  13.4 7.4 %all-to-all-start.1 = ((bf16[8,112,768]{2,1,0:T(8,128)(2,1)}), bf16[8,112,768]{2,1,0:T(8,128)(2,1)}, u32[]{:S(2)}, u32[]{:S(2)}) async-start(bf16[8,112,768]{2,1,0:T(8,128)(2,1)} %broadcast_select_fusion.1), calls=%async_computation.1 | async-start | bytes 2752512 | tf_op jit(solution)/shard_map/all_to_all | solution.py:690
  26.2 4.4 fusion
  32.0 21.7 %all-to-all-done.1 = bf16[8,112,768]{2,1,0:T(8,128)(2,1)} async-done(((bf16[8,112,768]{2,1,0:T(8,128)(2,1)}), bf16[8,112,768]{2,1,0:T(8,128)(2,1)}, u32[]{:S(2)}, u32[]{:S(2)}) %all-to-all-start.1) | async-done | bytes 1376288 | tf_op jit(solution)/shard_map/all_to_all | solution.py:690
  53.7 3.6 all-to-all-start
  58.5 3.3 copy.123
  63.8 20.3 %self_forward.1 = (bf16[2,256,768]{2,1,0:T(8,128)(2,1)}, bf16[2,256,2304]{2,1,0:T(8,128)(2,1)}, bf16[2,12,256,256]{3,2,1,0:T(8,128)(2,1)}, f32[2,16,256]{2,1,0:T...) custom-call(s32[2]{0:T(128)} %dec_len_ref.3, ...), custom_call_target="tpu_custom_call" | custom-call | flops 4831838208 | bytes 30000000 | tf_op jit(solution)/shard_map/self_forward/pallas_call | solution.py:468
  84.1 34.6 %cross_forward.2 = (bf16[2,256,768]{2,1,0:T(8,128)(2,1)}, bf16[2,896,1536]{2,1,0:T(8,128)(2,1)}, bf16[2,12,896,256]{3,2,1,0:T(8,128)(2,1)}, f32[2,16,256]{2,1,0:...) custom-call(s32[2]{0:T(128)} %and_select_fusion.mem_len_ref, ...), custom_call_target="tpu_custom_call" | custom-call | flops 11274289152 | bytes 30000000 | tf_op jit(solution)/shard_map/cross_forward/pallas_call | solution.py:441
  118.7 20.9 %cross_back.2 = (bf16[2,256,768]{2,1,0:T(8,128)(2,1)}, bf16[2,896,1536]{2,1,0:T(8,128)(2,1)}, bf16[2,896,768]{2,1,0:T(8,128)(2,1)}, f32[2,256,768]{2,1,0:T(8,128...) custom-call(bf16[2,256,768]{2,1,0:T(8,128)(2,1)} %get-tuple-element.100.rest_11_.branch_ref, ...), custom_call_target="tpu_custom_call" | custom-call | flops 8355053568 | bytes 30000000 | tf_op jit(solution)/shard_map/cross_back/pallas_call | solution.py:441
  140.8 34.5 %cross_forward.3 = (bf16[2,256,768]{2,1,0:T(8,128)(2,1)}, bf16[2,896,1536]{2,1,0:T(8,128)(2,1)}, bf16[2,12,896,256]{3,2,1,0:T(8,128)(2,1)}, f32[2,16,256]{2,1,0:...) custom-call(s32[2]{0:T(128)} %and_select_fusion.mem_len_ref, ...), custom_call_target="tpu_custom_call", output_to_operand_aliasing={{0}: (12, {}), {1}: (13, {}), {2}: (14, {}), {3}: (15, {}),... | custom-call | flops 11274289152 | bytes 30000000 | tf_op jit(solution)/shard_map/cross_forward/pallas_call | solution.py:441
  175.3 4.7 bitcast_convert_fusion
  194.1 20.9 %cross_back.3 = (bf16[2,256,768]{2,1,0:T(8,128)(2,1)}, bf16[2,896,1536]{2,1,0:T(8,128)(2,1)}, bf16[2,896,768]{2,1,0:T(8,128)(2,1)}, f32[2,256,768]{2,1,0:T(8,128...) custom-call(bf16[2,256,768]{2,1,0:T(8,128)(2,1)} %get-tuple-element., ...), custom_call_target="tpu_custom_call", output_to_operand_aliasing={{0}: (12, {}), {1}: (13, {}), {2}: (14, {}), {3}: (15, {}),... | custom-call | flops 8355053568 | bytes 30000000 | tf_op jit(solution)/shard_map/cross_back/pallas_call | solution.py:441
  215.0 5.0 fusion.6
  220.0 3.0 add_convert_fusion
  229.2 20.6 %self_back.1 = (bf16[2,256,2304]{2,1,0:T(8,128)(2,1)}, bf16[2,256,768]{2,1,0:T(8,128)(2,1)}, f32[2,24,768]{2,1,0:T(8,128)}, f32[2,16,512]{2,1,0:T(8,128)}) custom-call(bf16[2,256,768]{2,1,0:T(8,128)(2,1)} %get-tuple-element.116.branch_ref, f32[2,256,768]{2,1,0:T(8,128)} %get-tuple-element.117.gx2_ref, f32[2,256,768]{2,1,0:T(8,128)} %get-tuple-element.118.mixed_ref, ...), custom_call_target="tpu_custom_call" | custom-call | flops 4831838208 | bytes 30000000 | tf_op jit(solution)/shard_map/self_back/pallas_call | solution.py:543
  249.9 3.7 bitcast_convert_fusion.2
  290.1 6.1 all-to-all-start.3
  296.2 23.6 %all-reduce.4.cloned.1.call-done = f32[4,5888]{1,0:T(4,128)} async-done(((f32[4,5888]{1,0:T(4,128)}), f32[4,5888]{1,0:T(4,128)}) %all-reduce.4.cloned.1.call-update) | async-done | bytes 94224
  321.3 37.1 %psum.7 = f32[1,5888]{1,0:T(1,128)S(1)} all-reduce(f32[1,5888]{1,0:T(1,128)S(1)} %constant_dynamic-slice_fusion.1), channel_id=1, replica_groups=mesh['seq'=8,'grp'=4] {'seq'}, use_global_device_ids=true, to_apply=%region_7.9 | all-reduce | flops 5888 | bytes 47104 | tf_op jit(solution)/shard_map/psum | solution.py:766
  366.2 6.1 collective-permute-done.29
  372.3 5.8 collective-permute-done.15
  379.0 7.8 %collective-permute-done.8 = bf16[192,768]{1,0:T(8,128)(2,1)S(1)} collective-permute-done((bf16[192,768]{1,0:T(8,128)(2,1)S(1)}, bf16[192,768]{1,0:T(8,128)(2,1)S(1)}, u32[]{:S(2)}, u32[]{:S(2)}) %collective-permute-start.8) | collective-permute-done | bytes 294944 | tf_op jit(solution)/shard_map/ppermute | solution.py:608
  386.9 5.0 collective-permute-done.30
  392.0 6.0 collective-permute-done.16
  398.1 5.1 collective-permute-done.9
  408.2 4.4 collective-permute-start.10
  418.8 19.5 %collective-permute-done.33 = bf16[96,768]{1,0:T(8,128)(2,1)S(1)} collective-permute-done((bf16[96,768]{1,0:T(8,128)(2,1)S(1)}, bf16[96,768]{1,0:T(8,128)(2,1)S(1)}, u32[]{:S(2)}, u32[]{:S(2)}) %collective-permute-start.33) | collective-permute-done | bytes 147488 | tf_op jit(solution)/shard_map/ppermute | solution.py:617
  439.6 5.7 collective-permute-done.19
  446.7 5.7 collective-permute-done.12
  452.4 6.7 %collective-permute-done.34 = bf16[96,768]{1,0:T(8,128)(2,1)S(1)} collective-permute-done((bf16[96,768]{1,0:T(8,128)(2,1)S(1)}, bf16[96,768]{1,0:T(8,128)(2,1)S(1)}, u32[]{:S(2)}, u32[]{:S(2)}) %collective-permute-start.34) | collective-permute-done | bytes 147488 | tf_op jit(solution)/shard_map/ppermute | solution.py:620
  459.1 5.1 collective-permute-done.20
  466.0 6.1 collective-permute-done.13
  476.4 4.4 all-to-all-start.2
  481.9 4.1 collective-permute-start.24
  486.0 2.9 fusion.2
  497.7 5.0 all-to-all-done.2
  507.1 3.8 broadcast_select_fusion
  515.2 5.8 collective-permute-done.26
  522.5 4.1 collective-permute-done.2
  526.7 5.0 collective-permute-start.3
  546.0 4.9 collective-permute-start.45
  552.3 4.9 collective-permute-start.38
  559.5 5.1 collective-permute-done.38
  565.4 6.0 collective-permute-done.5
  575.7 7.5 %collective-permute-done.6 = bf16[96,2304]{1,0:T(8,128)(2,1)S(1)} collective-permute-done((bf16[96,2304]{1,0:T(8,128)(2,1)S(1)}, bf16[96,2304]{1,0:T(8,128)(2,1)S(1)}, u32[]{:S(2)}, u32[]{:S(2)}) %collective-permute-start.6) | collective-permute-done | bytes 442400 | tf_op jit(solution)/shard_map/ppermute | solution.py:620
  583.3 3.2 collective-permute-done.47
  588.0 4.8 collective-permute-done.40
  595.6 3.2 collective-permute-done.48
  600.4 4.7 collective-permute-done.41
  (391 shorter events, 154.7 us)
Async XLA Ops:
  13.4 40.3 %all-to-all-start.1 = ((bf16[8,112,768]{2,1,0:T(8,128)(2,1)}), bf16[8,112,768]{2,1,0:T(8,128)(2,1)}, u32[]{:S(2)}, u32[]{:S(2)}) async-start(bf16[8,112,768]{2,1,0:T(8,128)(2,1)} %broadcast_select_fusion.1), calls=%async_computation.1 | async-start | bytes 2752512 | tf_op jit(solution)/shard_map/all_to_all | solution.py:690
  53.7 86.0 %all-to-all-start = ((bf16[8,112,768]{2,1,0:T(8,128)(2,1)}), bf16[8,112,768]{2,1,0:T(8,128)(2,1)S(1)}, u32[]{:S(2)}, u32[]{:S(2)}) async-start(bf16[8,112,768]{2,1,0:T(8,128)(2,1)} %broadcast_select_fusion.2), calls=%async_computation | async-start | bytes 2752512 | tf_op jit(solution)/shard_map/all_to_all | solution.py:690
  57.3 262.5 %all-reduce.4.cloned.1.call-start = ((), (), s32[]{:S(2)}) async-start(), calls=%async_computation.4 | async-start | bytes 188416
  183.6 302.4 %collective-permute-start.42 = (bf16[2,768,768]{2,1,0:T(8,128)(2,1)}, bf16[2,768,768]{2,1,0:T(8,128)(2,1)}, u32[]{:S(2)}, u32[]{:S(2)}) collective-permute-start(bf16[2,768,768]{2,1,0:T(8,128)(2,1)} %dynamic-slice_bitcast_fusion), channel_id=1, source_target_pairs={{0,1},{1,0},{2,3},{3,2},{4,5},{5,4},{6,7},{7,6},{8,9},{9,8},{10,11... | collective-permute-start | bytes 7077896 | tf_op jit(solution)/shard_map/ppermute | solution.py:606
  190.4 301.2 %collective-permute-start.35 = (bf16[2,192,3072]{2,1,0:T(8,128)(2,1)}, bf16[2,192,3072]{2,1,0:T(8,128)(2,1)}, u32[]{:S(2)}, u32[]{:S(2)}) collective-permute-start(bf16[2,192,3072]{2,1,0:T(8,128)(2,1)} %dynamic-slice_bitcast_fusion.1), channel_id=1, source_target_pairs={{0,1},{1,0},{2,3},{3,2},{4,5},{5,4},{6,7},{7,6},{8,9},{9,8},{10,11... | collective-permute-start | bytes 7077896 | tf_op jit(solution)/shard_map/ppermute | solution.py:606
  192.3 168.8 %collective-permute-start.28 = (bf16[2,192,768]{2,1,0:T(8,128)(2,1)S(1)}, bf16[2,192,768]{2,1,0:T(8,128)(2,1)}, u32[]{:S(2)}, u32[]{:S(2)}) collective-permute-start(bf16[2,192,768]{2,1,0:T(8,128)(2,1)S(1)} %dynamic-slice_bitcast_fusion.9), channel_id=1, source_target_pairs={{0,1},{1,0},{2,3},{3,2},{4,5},{5,4},{6,7},{7,6},{8,9},{9,8},{10,11... | collective-permute-start | bytes 1769480 | tf_op jit(solution)/shard_map/ppermute | solution.py:606
  224.2 180.3 %collective-permute-start.21 = (bf16[2,192,1536]{2,1,0:T(8,128)(2,1)}, bf16[2,192,1536]{2,1,0:T(8,128)(2,1)}, u32[]{:S(2)}, u32[]{:S(2)}) collective-permute-start(bf16[2,192,1536]{2,1,0:T(8,128)(2,1)} %dynamic-slice_bitcast_fusion.5), channel_id=1, source_target_pairs={{0,1},{1,0},{2,3},{3,2},{4,5},{5,4},{6,7},{7,6},{8,9},{9,8},{10,11... | collective-permute-start | bytes 3538952 | tf_op jit(solution)/shard_map/ppermute | solution.py:606
  227.3 135.0 %collective-permute-start.14 = (bf16[2,192,768]{2,1,0:T(8,128)(2,1)}, bf16[2,192,768]{2,1,0:T(8,128)(2,1)}, u32[]{:S(2)}, u32[]{:S(2)}) collective-permute-start(bf16[2,192,768]{2,1,0:T(8,128)(2,1)} %dynamic-slice_bitcast_fusion.11), channel_id=1, source_target_pairs={{0,1},{1,0},{2,3},{3,2},{4,5},{5,4},{6,7},{7,6},{8,9},{9,8},{10,11... | collective-permute-start | bytes 1769480 | tf_op jit(solution)/shard_map/ppermute | solution.py:606
  290.1 186.3 %all-to-all-start.3 = ((bf16[8,112,768]{2,1,0:T(8,128)(2,1)}), bf16[8,112,768]{2,1,0:T(8,128)(2,1)}, u32[]{:S(2)}, u32[]{:S(2)}) async-start(bf16[8,112,768]{2,1,0:T(8,128)(2,1)} %bitcast.196), calls=%async_computation.3 | async-start | bytes 2752512 | tf_op jit(solution)/shard_map/all_to_all | solution.py:726
  362.4 9.9 %collective-permute-start.29 = (bf16[192,768]{1,0:T(8,128)(2,1)S(1)}, bf16[192,768]{1,0:T(8,128)(2,1)S(1)}, u32[]{:S(2)}, u32[]{:S(2)}) collective-permute-start(bf16[192,768]{1,0:T(8,128)(2,1)S(1)} %dynamic-slice_bitcast_fusion.14), channel_id=1, source_target_pairs={{0,2},{2,0},{1,3},{3,1},{4,6},{6,4},{5,7},{7,5},{8,10},{10,8},{9,1... | collective-permute-start | bytes 884744 | tf_op jit(solution)/shard_map/ppermute | solution.py:608
  364.6 13.6 %collective-permute-start.15 = (bf16[192,768]{1,0:T(8,128)(2,1)S(1)}, bf16[192,768]{1,0:T(8,128)(2,1)S(1)}, u32[]{:S(2)}, u32[]{:S(2)}) collective-permute-start(bf16[192,768]{1,0:T(8,128)(2,1)S(1)} %dynamic-slice_bitcast_fusion.16), channel_id=1, source_target_pairs={{0,2},{2,0},{1,3},{3,1},{4,6},{6,4},{5,7},{7,5},{8,10},{10,8},{9,1... | collective-permute-start | bytes 884744 | tf_op jit(solution)/shard_map/ppermute | solution.py:608
  372.3 101.1 %collective-permute-start = (bf16[2,192,2304]{2,1,0:T(8,128)(2,1)S(1)}, bf16[2,192,2304]{2,1,0:T(8,128)(2,1)S(1)}, u32[]{:S(2)}, u32[]{:S(2)}) collective-permute-start(bf16[2,192,2304]{2,1,0:T(8,128)(2,1)S(1)} %copy-done.23), channel_id=1, source_target_pairs={{0,1},{1,0},{2,3},{3,2},{4,5},{5,4},{6,7},{7,6},{8,9},{9,8},{10,11... | collective-permute-start | bytes 5308424 | tf_op jit(solution)/shard_map/ppermute | solution.py:606
  378.2 8.6 %collective-permute-start.8 = (bf16[192,768]{1,0:T(8,128)(2,1)S(1)}, bf16[192,768]{1,0:T(8,128)(2,1)S(1)}, u32[]{:S(2)}, u32[]{:S(2)}) collective-permute-start(bf16[192,768]{1,0:T(8,128)(2,1)S(1)} %dynamic-slice_bitcast_fusion.17), channel_id=1, source_target_pairs={{0,2},{2,0},{1,3},{3,1},{4,6},{6,4},{5,7},{7,5},{8,10},{10,8},{9,1... | collective-permute-start | bytes 884744 | tf_op jit(solution)/shard_map/ppermute | solution.py:608
  386.8 5.1 collective-permute-start.30
  391.9 6.1 collective-permute-start.16
  398.0 5.1 collective-permute-start.9
  404.5 8.1 %collective-permute-start.17 = (bf16[96,768]{1,0:T(8,128)(2,1)S(1)}, bf16[96,768]{1,0:T(8,128)(2,1)S(1)}, u32[]{:S(2)}, u32[]{:S(2)}) collective-permute-start(bf16[96,768]{1,0:T(8,128)(2,1)S(1)} %fusion.27), channel_id=1, source_target_pairs={{0,8},{4,12},{24,16},{28,20},{1,9},{5,13},{25,17},{29,21},{2,10},{... | collective-permute-start | bytes 442376 | tf_op jit(solution)/shard_map/ppermute | solution.py:613
  408.2 7.0 %collective-permute-start.10 = (bf16[96,768]{1,0:T(8,128)(2,1)S(1)}, bf16[96,768]{1,0:T(8,128)(2,1)S(1)}, u32[]{:S(2)}, u32[]{:S(2)}) collective-permute-start(bf16[96,768]{1,0:T(8,128)(2,1)S(1)} %fusion.28), channel_id=1, source_target_pairs={{0,8},{4,12},{24,16},{28,20},{1,9},{5,13},{25,17},{29,21},{2,10},{... | collective-permute-start | bytes 442376 | tf_op jit(solution)/shard_map/ppermute | solution.py:613
  415.3 57.7 %collective-permute-start.22 = (bf16[192,1536]{1,0:T(8,128)(2,1)S(1)}, bf16[192,1536]{1,0:T(8,128)(2,1)S(1)}, u32[]{:S(2)}, u32[]{:S(2)}) collective-permute-start(bf16[192,1536]{1,0:T(8,128)(2,1)S(1)} %dynamic-slice_bitcast_fusion.10), channel_id=1, source_target_pairs={{0,2},{2,0},{1,3},{3,1},{4,6},{6,4},{5,7},{7,5},{8,10},{10,8},{9,1... | collective-permute-start | bytes 1769480 | tf_op jit(solution)/shard_map/ppermute | solution.py:608
  417.4 20.9 %collective-permute-start.33 = (bf16[96,768]{1,0:T(8,128)(2,1)S(1)}, bf16[96,768]{1,0:T(8,128)(2,1)S(1)}, u32[]{:S(2)}, u32[]{:S(2)}) collective-permute-start(bf16[96,768]{1,0:T(8,128)(2,1)S(1)} %add_convert_fusion.9), channel_id=1, source_target_pairs={{8,0},{12,4},{16,24},{20,28},{9,1},{13,5},{17,25},{21,29},{10,2},{... | collective-permute-start | bytes 442376 | tf_op jit(solution)/shard_map/ppermute | solution.py:617
  438.3 7.0 %collective-permute-start.19 = (bf16[96,768]{1,0:T(8,128)(2,1)S(1)}, bf16[96,768]{1,0:T(8,128)(2,1)S(1)}, u32[]{:S(2)}, u32[]{:S(2)}) collective-permute-start(bf16[96,768]{1,0:T(8,128)(2,1)S(1)} %add_convert_fusion.11), channel_id=1, source_target_pairs={{8,0},{12,4},{16,24},{20,28},{9,1},{13,5},{17,25},{21,29},{10,2},{... | collective-permute-start | bytes 442376 | tf_op jit(solution)/shard_map/ppermute | solution.py:617
  445.4 7.0 %collective-permute-start.12 = (bf16[96,768]{1,0:T(8,128)(2,1)S(1)}, bf16[96,768]{1,0:T(8,128)(2,1)S(1)}, u32[]{:S(2)}, u32[]{:S(2)}) collective-permute-start(bf16[96,768]{1,0:T(8,128)(2,1)S(1)} %add_convert_fusion.13), channel_id=1, source_target_pairs={{8,0},{12,4},{16,24},{20,28},{9,1},{13,5},{17,25},{21,29},{10,2},{... | collective-permute-start | bytes 442376 | tf_op jit(solution)/shard_map/ppermute | solution.py:617
  452.4 6.7 %collective-permute-start.34 = (bf16[96,768]{1,0:T(8,128)(2,1)S(1)}, bf16[96,768]{1,0:T(8,128)(2,1)S(1)}, u32[]{:S(2)}, u32[]{:S(2)}) collective-permute-start(bf16[96,768]{1,0:T(8,128)(2,1)S(1)} %broadcast_select_fusion.15), channel_id=1, source_target_pairs={{0,4},{4,0},{8,12},{12,8},{16,20},{20,16},{24,28},{28,24},{1,5},{5... | collective-permute-start | bytes 442376 | tf_op jit(solution)/shard_map/ppermute | solution.py:620
  464.2 7.8 %collective-permute-start.13 = (bf16[96,768]{1,0:T(8,128)(2,1)S(1)}, bf16[96,768]{1,0:T(8,128)(2,1)S(1)}, u32[]{:S(2)}, u32[]{:S(2)}) collective-permute-start(bf16[96,768]{1,0:T(8,128)(2,1)S(1)} %broadcast_select_fusion.17), channel_id=1, source_target_pairs={{0,4},{4,0},{8,12},{12,8},{16,20},{20,16},{24,28},{28,24},{1,5},{5... | collective-permute-start | bytes 442376 | tf_op jit(solution)/shard_map/ppermute | solution.py:620
  473.1 7.7 %collective-permute-start.23 = (bf16[96,1536]{1,0:T(8,128)(2,1)S(1)}, bf16[96,1536]{1,0:T(8,128)(2,1)}, u32[]{:S(2)}, u32[]{:S(2)}) collective-permute-start(bf16[96,1536]{1,0:T(8,128)(2,1)S(1)} %dynamic-slice_bitcast_fusion.15), channel_id=1, source_target_pairs={{0,4},{4,0},{8,12},{12,8},{16,20},{20,16},{24,28},{28,24},{1,5},{5... | collective-permute-start | bytes 884744 | tf_op jit(solution)/shard_map/ppermute | solution.py:611
  475.8 35.1 %collective-permute-start.1 = (bf16[192,2304]{1,0:T(8,128)(2,1)}, bf16[192,2304]{1,0:T(8,128)(2,1)}, u32[]{:S(2)}, u32[]{:S(2)}) collective-permute-start(bf16[192,2304]{1,0:T(8,128)(2,1)} %dynamic-slice_bitcast_fusion.6), channel_id=1, source_target_pairs={{0,2},{2,0},{1,3},{3,1},{4,6},{6,4},{5,7},{7,5},{8,10},{10,8},{9,1... | collective-permute-start | bytes 2654216 | tf_op jit(solution)/shard_map/ppermute | solution.py:608
  476.4 26.3 %all-to-all-start.2 = ((bf16[8,112,768]{2,1,0:T(8,128)(2,1)}), bf16[8,112,768]{2,1,0:T(8,128)(2,1)}, u32[]{:S(2)}, u32[]{:S(2)}) async-start(bf16[8,112,768]{2,1,0:T(8,128)(2,1)} %bitcast.195), calls=%async_computation.2 | async-start | bytes 2752512 | tf_op jit(solution)/shard_map/all_to_all | solution.py:726
  481.9 14.9 %collective-permute-start.24 = (bf16[96,1536]{1,0:T(8,128)(2,1)S(1)}, bf16[96,1536]{1,0:T(8,128)(2,1)S(1)}, u32[]{:S(2)}, u32[]{:S(2)}) collective-permute-start(bf16[96,1536]{1,0:T(8,128)(2,1)S(1)} %fusion.23), channel_id=1, source_target_pairs={{0,8},{4,12},{24,16},{28,20},{1,9},{5,13},{25,17},{29,21},{2,10},{... | collective-permute-start | bytes 884744 | tf_op jit(solution)/shard_map/ppermute | solution.py:613
  490.2 43.9 %collective-permute-start.43 = (bf16[768,768]{1,0:T(8,128)(2,1)}, bf16[768,768]{1,0:T(8,128)(2,1)}, u32[]{:S(2)}, u32[]{:S(2)}) collective-permute-start(bf16[768,768]{1,0:T(8,128)(2,1)} %dynamic-slice_bitcast_fusion.3), channel_id=1, source_target_pairs={{0,2},{2,0},{1,3},{3,1},{4,6},{6,4},{5,7},{7,5},{8,10},{10,8},{9,1... | collective-permute-start | bytes 3538952 | tf_op jit(solution)/shard_map/ppermute | solution.py:608
  495.4 42.2 %collective-permute-start.36 = (bf16[192,3072]{1,0:T(8,128)(2,1)}, bf16[192,3072]{1,0:T(8,128)(2,1)}, u32[]{:S(2)}, u32[]{:S(2)}) collective-permute-start(bf16[192,3072]{1,0:T(8,128)(2,1)} %dynamic-slice_bitcast_fusion.4), channel_id=1, source_target_pairs={{0,2},{2,0},{1,3},{3,1},{4,6},{6,4},{5,7},{7,5},{8,10},{10,8},{9,1... | collective-permute-start | bytes 3538952 | tf_op jit(solution)/shard_map/ppermute | solution.py:608
  496.8 15.5 %collective-permute-start.25 = (bf16[96,1536]{1,0:T(8,128)(2,1)S(1)}, bf16[96,1536]{1,0:T(8,128)(2,1)S(1)}, u32[]{:S(2)}, u32[]{:S(2)}) collective-permute-start(bf16[96,1536]{1,0:T(8,128)(2,1)S(1)} %add_convert_fusion.8), channel_id=1, source_target_pairs={{8,16},{16,8},{12,20},{20,12},{9,17},{17,9},{13,21},{21,13},{10,18... | collective-permute-start | bytes 884744 | tf_op jit(solution)/shard_map/ppermute | solution.py:615
  512.4 8.6 %collective-permute-start.26 = (bf16[96,1536]{1,0:T(8,128)(2,1)S(1)}, bf16[96,1536]{1,0:T(8,128)(2,1)S(1)}, u32[]{:S(2)}, u32[]{:S(2)}) collective-permute-start(bf16[96,1536]{1,0:T(8,128)(2,1)S(1)} %add_convert_fusion.7), channel_id=1, source_target_pairs={{8,0},{12,4},{16,24},{20,28},{9,1},{13,5},{17,25},{21,29},{10,2},{... | collective-permute-start | bytes 884744 | tf_op jit(solution)/shard_map/ppermute | solution.py:617
  513.7 12.9 %collective-permute-start.2 = (bf16[96,2304]{1,0:T(8,128)(2,1)S(1)}, bf16[96,2304]{1,0:T(8,128)(2,1)S(1)}, u32[]{:S(2)}, u32[]{:S(2)}) collective-permute-start(bf16[96,2304]{1,0:T(8,128)(2,1)S(1)} %dynamic-slice_bitcast_fusion.13), channel_id=1, source_target_pairs={{0,4},{4,0},{8,12},{12,8},{16,20},{20,16},{24,28},{28,24},{1,5},{5... | collective-permute-start | bytes 1327112 | tf_op jit(solution)/shard_map/ppermute | solution.py:611
  521.0 11.9 %collective-permute-start.27 = (bf16[96,1536]{1,0:T(8,128)(2,1)S(1)}, bf16[96,1536]{1,0:T(8,128)(2,1)S(1)}, u32[]{:S(2)}, u32[]{:S(2)}) collective-permute-start(bf16[96,1536]{1,0:T(8,128)(2,1)S(1)} %broadcast_select_fusion.12), channel_id=1, source_target_pairs={{0,4},{4,0},{8,12},{12,8},{16,20},{20,16},{24,28},{28,24},{1,5},{5... | collective-permute-start | bytes 884744 | tf_op jit(solution)/shard_map/ppermute | solution.py:620
  526.7 15.5 %collective-permute-start.3 = (bf16[96,2304]{1,0:T(8,128)(2,1)S(1)}, bf16[96,2304]{1,0:T(8,128)(2,1)S(1)}, u32[]{:S(2)}, u32[]{:S(2)}) collective-permute-start(bf16[96,2304]{1,0:T(8,128)(2,1)S(1)} %fusion.21), channel_id=1, source_target_pairs={{0,8},{4,12},{24,16},{28,20},{1,9},{5,13},{25,17},{29,21},{2,10},{... | collective-permute-start | bytes 1327112 | tf_op jit(solution)/shard_map/ppermute | solution.py:613
  535.9 9.9 %collective-permute-start.44 = (bf16[384,768]{1,0:T(8,128)(2,1)S(1)}, bf16[384,768]{1,0:T(8,128)(2,1)S(1)}, u32[]{:S(2)}, u32[]{:S(2)}) collective-permute-start(bf16[384,768]{1,0:T(8,128)(2,1)S(1)} %dynamic-slice_bitcast_fusion.7), channel_id=1, source_target_pairs={{0,4},{4,0},{8,12},{12,8},{16,20},{20,16},{24,28},{28,24},{1,5},{5... | collective-permute-start | bytes 1769480 | tf_op jit(solution)/shard_map/ppermute | solution.py:611
  539.3 12.9 %collective-permute-start.37 = (bf16[96,3072]{1,0:T(8,128)(2,1)S(1)}, bf16[96,3072]{1,0:T(8,128)(2,1)S(1)}, u32[]{:S(2)}, u32[]{:S(2)}) collective-permute-start(bf16[96,3072]{1,0:T(8,128)(2,1)S(1)} %dynamic-slice_bitcast_fusion.8), channel_id=1, source_target_pairs={{0,4},{4,0},{8,12},{12,8},{16,20},{20,16},{24,28},{28,24},{1,5},{5... | collective-permute-start | bytes 1769480 | tf_op jit(solution)/shard_map/ppermute | solution.py:611
  542.3 14.9 %collective-permute-start.4 = (bf16[96,2304]{1,0:T(8,128)(2,1)S(1)}, bf16[96,2304]{1,0:T(8,128)(2,1)S(1)}, u32[]{:S(2)}, u32[]{:S(2)}) collective-permute-start(bf16[96,2304]{1,0:T(8,128)(2,1)S(1)} %add_convert_fusion.6), channel_id=1, source_target_pairs={{8,16},{16,8},{12,20},{20,12},{9,17},{17,9},{13,21},{21,13},{10,18... | collective-permute-start | bytes 1327112 | tf_op jit(solution)/shard_map/ppermute | solution.py:615
  546.0 12.7 %collective-permute-start.45 = (bf16[384,768]{1,0:T(8,128)(2,1)S(1)}, bf16[384,768]{1,0:T(8,128)(2,1)S(1)}, u32[]{:S(2)}, u32[]{:S(2)}) collective-permute-start(bf16[384,768]{1,0:T(8,128)(2,1)S(1)} %fusion.15), channel_id=1, source_target_pairs={{0,8},{4,12},{24,16},{28,20},{1,9},{5,13},{25,17},{29,21},{2,10},{... | collective-permute-start | bytes 1769480 | tf_op jit(solution)/shard_map/ppermute | solution.py:613
  552.3 12.3 %collective-permute-start.38 = (bf16[96,3072]{1,0:T(8,128)(2,1)S(1)}, bf16[96,3072]{1,0:T(8,128)(2,1)S(1)}, u32[]{:S(2)}, u32[]{:S(2)}) collective-permute-start(bf16[96,3072]{1,0:T(8,128)(2,1)S(1)} %fusion.16), channel_id=1, source_target_pairs={{0,8},{4,12},{24,16},{28,20},{1,9},{5,13},{25,17},{29,21},{2,10},{... | collective-permute-start | bytes 1769480 | tf_op jit(solution)/shard_map/ppermute | solution.py:613
  557.3 14.1 %collective-permute-start.5 = (bf16[96,2304]{1,0:T(8,128)(2,1)S(1)}, bf16[96,2304]{1,0:T(8,128)(2,1)S(1)}, u32[]{:S(2)}, u32[]{:S(2)}) collective-permute-start(bf16[96,2304]{1,0:T(8,128)(2,1)S(1)} %add_convert_fusion.5), channel_id=1, source_target_pairs={{8,0},{12,4},{16,24},{20,28},{9,1},{13,5},{17,25},{21,29},{10,2},{... | collective-permute-start | bytes 1327112 | tf_op jit(solution)/shard_map/ppermute | solution.py:617
  558.8 14.0 %collective-permute-start.46 = (bf16[384,768]{1,0:T(8,128)(2,1)S(1)}, bf16[384,768]{1,0:T(8,128)(2,1)S(1)}, u32[]{:S(2)}, u32[]{:S(2)}) collective-permute-start(bf16[384,768]{1,0:T(8,128)(2,1)S(1)} %add_convert_fusion.2), channel_id=1, source_target_pairs={{8,16},{16,8},{12,20},{20,12},{9,17},{17,9},{13,21},{21,13},{10,18... | collective-permute-start | bytes 1769480 | tf_op jit(solution)/shard_map/ppermute | solution.py:615
  564.7 9.5 %collective-permute-start.39 = (bf16[96,3072]{1,0:T(8,128)(2,1)S(1)}, bf16[96,3072]{1,0:T(8,128)(2,1)S(1)}, u32[]{:S(2)}, u32[]{:S(2)}) collective-permute-start(bf16[96,3072]{1,0:T(8,128)(2,1)S(1)} %add_convert_fusion.4), channel_id=1, source_target_pairs={{8,16},{16,8},{12,20},{20,12},{9,17},{17,9},{13,21},{21,13},{10,18... | collective-permute-start | bytes 1769480 | tf_op jit(solution)/shard_map/ppermute | solution.py:615
  571.5 11.7 %collective-permute-start.6 = (bf16[96,2304]{1,0:T(8,128)(2,1)S(1)}, bf16[96,2304]{1,0:T(8,128)(2,1)S(1)}, u32[]{:S(2)}, u32[]{:S(2)}) collective-permute-start(bf16[96,2304]{1,0:T(8,128)(2,1)S(1)} %broadcast_select_fusion.9), channel_id=1, source_target_pairs={{0,4},{4,0},{8,12},{12,8},{16,20},{20,16},{24,28},{28,24},{1,5},{5... | collective-permute-start | bytes 1327112 | tf_op jit(solution)/shard_map/ppermute | solution.py:620
  572.9 13.6 %collective-permute-start.47 = (bf16[384,768]{1,0:T(8,128)(2,1)S(1)}, bf16[384,768]{1,0:T(8,128)(2,1)S(1)}, u32[]{:S(2)}, u32[]{:S(2)}) collective-permute-start(bf16[384,768]{1,0:T(8,128)(2,1)S(1)} %add_convert_fusion.1), channel_id=1, source_target_pairs={{8,0},{12,4},{16,24},{20,28},{9,1},{13,5},{17,25},{21,29},{10,2},{... | collective-permute-start | bytes 1769480 | tf_op jit(solution)/shard_map/ppermute | solution.py:617
  574.4 18.4 %collective-permute-start.40 = (bf16[96,3072]{1,0:T(8,128)(2,1)S(1)}, bf16[96,3072]{1,0:T(8,128)(2,1)S(1)}, u32[]{:S(2)}, u32[]{:S(2)}) collective-permute-start(bf16[96,3072]{1,0:T(8,128)(2,1)S(1)} %add_convert_fusion.3), channel_id=1, source_target_pairs={{8,0},{12,4},{16,24},{20,28},{9,1},{13,5},{17,25},{21,29},{10,2},{... | collective-permute-start | bytes 1769480 | tf_op jit(solution)/shard_map/ppermute | solution.py:617
  586.6 12.2 %collective-permute-start.48 = (bf16[384,768]{1,0:T(8,128)(2,1)S(1)}, bf16[384,768]{1,0:T(8,128)(2,1)S(1)}, u32[]{:S(2)}, u32[]{:S(2)}) collective-permute-start(bf16[384,768]{1,0:T(8,128)(2,1)S(1)} %broadcast_select_fusion.3), channel_id=1, source_target_pairs={{0,4},{4,0},{8,12},{12,8},{16,20},{20,16},{24,28},{28,24},{1,5},{5... | collective-permute-start | bytes 1769480 | tf_op jit(solution)/shard_map/ppermute | solution.py:620
  592.9 12.2 %collective-permute-start.41 = (bf16[96,3072]{1,0:T(8,128)(2,1)S(1)}, bf16[96,3072]{1,0:T(8,128)(2,1)S(1)}, u32[]{:S(2)}, u32[]{:S(2)}) collective-permute-start(bf16[96,3072]{1,0:T(8,128)(2,1)S(1)} %broadcast_select_fusion.6), channel_id=1, source_target_pairs={{0,4},{4,0},{8,12},{12,8},{16,20},{20,16},{24,28},{28,24},{1,5},{5... | collective-permute-start | bytes 1769480 | tf_op jit(solution)/shard_map/ppermute | solution.py:620
  (73 other events, 790.1 us)
Sparse Core Ops, SparseCore 0:
  287.1 32.6 all-reduce.3
